TPU v7x, 256 devices: a whole 4x4x8 slice. The times are simulated.
256 devices in a mesh: prompt: 8 (over z), sample: 4 (over y), head: 8 (over x, core).
Axes of the slice: x: 4, y: 4, z: 8, core: 2. Of those that a mesh axis runs over, the one named last changes fastest.
Arguments:
- q_nope: bfloat16 [384, 2, 12288], P(('prompt', 'sample'), None, 'head'), may hold values from -3 to 3
- q_rope: bfloat16 [384, 2, 6144], P(('prompt', 'sample'), None, 'head'), may hold values from -24 to 24
- new_latent: bfloat16 [384, 2, 512], P(('prompt', 'sample')), may hold values from -4 to 4
- new_rope: bfloat16 [384, 2, 64], P(('prompt', 'sample')), may hold values from -4 to 4
- prompt_latent: bfloat16 [32, 2048, 512], P(('prompt', 'sample')), may hold values from -4 to 4
- prompt_rope: bfloat16 [32, 64, 2048], P(('prompt', 'sample')), may hold values from -4 to 4
- suffix_latent: bfloat16 [384, 128, 512], P(('prompt', 'sample')), may hold values from -4 to 4
- suffix_rope: bfloat16 [384, 64, 128], P(('prompt', 'sample')), may hold values from -4 to 4
- sample_prompt: int32 [384], P(('prompt', 'sample')), may hold values from 0 to 31, as said below
- suffix_len: int32 [384], P(('prompt', 'sample')), may hold values from 1 to 128, 24576 in all
- w_uk: bfloat16 [96, 128, 512], P('head'), may hold values from -0.5 to 0.5
- w_uv: bfloat16 [96, 512, 128], P('head'), may hold values from -1 to 1
- w_out: bfloat16 [12288, 7168], P('head', 'sample'), may hold values from -0.109375 to 0.109375
Outputs:
- layer_output: bfloat16 [384, 2, 7168], P('prompt', None, ('sample', 'head'))
Inputs may be any that keep to these rules, and one draw needn't show every extreme that they name: `sample_prompt`: the rows of one device of prompt and sample name 12 different prompts. A prompt is named by at most 16 samples, and some prompt by exactly that many.
All inputs are finite; a program needn't handle non-finite values. No bound on the sum of `suffix_len` on one device may be relied on, other than what follows from the above.
Results may differ from a plain program's by a relative error of at most 0.0066.
Values may be sent and summed in bfloat16 or wider, within the bound.
A program may use at most 64 MiB of HBM per device.

v0:
```python
import math

import jax
import jax.numpy as jnp
from jax import lax
from jax.sharding import PartitionSpec as P

NOPE = 128
ROPE = 64
LAT = 512
VDIM = 128


def shards(
    q_nope,
    q_rope,
    new_latent,
    new_rope,
    prompt_latent,
    prompt_rope,
    suffix_latent,
    suffix_rope,
    sample_prompt,
    suffix_len,
    w_uk,
    w_uv,
    w_out,
):
    row_count = q_nope.shape[0]
    head_count = w_uk.shape[0]
    suffix_count = suffix_latent.shape[1]
    score_scale = 1.0 / math.sqrt(NOPE + ROPE)
    outer_count = lax.axis_size("prompt")
    inner_count = lax.axis_size("sample")
    owner_count = outer_count * inner_count
    floor_value = -1e30
    queries_nope = q_nope.reshape(row_count, 2, head_count, NOPE)
    queries_rope = q_rope.reshape(row_count, 2, head_count, ROPE)
    queries_lat = jnp.einsum(
        "sthn,hnl->sthl", queries_nope, w_uk, preferred_element_type=jnp.float32
    ).astype(jnp.bfloat16)
    cache_latent = prompt_latent[0]
    cache_rope = prompt_rope[0]
    selector = (sample_prompt[None, :] == jnp.arange(owner_count, dtype=jnp.int32)[:, None]).astype(
        jnp.bfloat16
    )

    def place_rows(source):
        return jnp.einsum(
            "ps,sthx->pthx", selector, source, preferred_element_type=jnp.float32
        ).astype(jnp.bfloat16)

    lead_send = place_rows(queries_lat)
    rope_send = place_rows(queries_rope)
    lead_part = lax.all_to_all(
        lead_send, ("prompt", "sample"), split_axis=0, concat_axis=0, tiled=True
    )
    slot_count = lead_part.shape[0]
    item_count = lead_part.shape[1]
    flat_lat = lead_part.reshape(-1, LAT)
    flat_rope = lax.all_to_all(
        rope_send, ("prompt", "sample"), split_axis=0, concat_axis=0, tiled=True
    ).reshape(-1, ROPE)
    scores = (
        jnp.einsum("rx,kx->rk", flat_lat, cache_latent, preferred_element_type=jnp.float32)
        + jnp.dot(flat_rope, cache_rope, preferred_element_type=jnp.float32)
    ) * score_scale
    row_peak = jnp.max(scores, axis=-1)
    expo_vals = jnp.exp(scores - row_peak[:, None])
    totals = jnp.sum(expo_vals, axis=-1)
    weighted = jnp.dot(
        expo_vals.astype(jnp.bfloat16), cache_latent, preferred_element_type=jnp.float32
    )
    prefix_out = jnp.take(
        lax.all_to_all(
            weighted.reshape(slot_count, item_count, head_count, LAT),
            ("prompt", "sample"),
            split_axis=0,
            concat_axis=0,
            tiled=True,
        ),
        sample_prompt,
        axis=0,
    ).reshape(row_count, 2 * head_count, LAT)
    prefix_peak = jnp.take(
        lax.all_to_all(
            row_peak.reshape(slot_count, item_count, head_count),
            ("prompt", "sample"),
            split_axis=0,
            concat_axis=0,
            tiled=True,
        ),
        sample_prompt,
        axis=0,
    ).reshape(row_count, 2 * head_count)
    prefix_total = jnp.take(
        lax.all_to_all(
            totals.reshape(slot_count, item_count, head_count),
            ("prompt", "sample"),
            split_axis=0,
            concat_axis=0,
            tiled=True,
        ),
        sample_prompt,
        axis=0,
    ).reshape(row_count, 2 * head_count)
    lat_rows = queries_lat.reshape(row_count, 2 * head_count, LAT)
    rope_rows = queries_rope.reshape(row_count, 2 * head_count, ROPE)
    suffix_scores = (
        jnp.einsum("sqx,skx->sqk", lat_rows, suffix_latent, preferred_element_type=jnp.float32)
        + jnp.einsum("sqx,sxk->sqk", rope_rows, suffix_rope, preferred_element_type=jnp.float32)
    ) * score_scale
    new_scores = (
        jnp.einsum("sqx,skx->sqk", lat_rows, new_latent, preferred_element_type=jnp.float32)
        + jnp.einsum("sqx,skx->sqk", rope_rows, new_rope, preferred_element_type=jnp.float32)
    ) * score_scale
    suffix_valid = (
        jnp.arange(suffix_count, dtype=jnp.int32)[None, None, :] < suffix_len[:, None, None]
    )
    token_of = jnp.arange(2 * head_count, dtype=jnp.int32) // head_count
    new_valid = jnp.arange(2, dtype=jnp.int32)[None, None, :] <= token_of[None, :, None]
    local_peak = jnp.maximum(
        jnp.max(jnp.where(suffix_valid, suffix_scores, floor_value), axis=-1),
        jnp.max(jnp.where(new_valid, new_scores, floor_value), axis=-1),
    )
    suffix_exp = jnp.where(suffix_valid, jnp.exp(suffix_scores - local_peak[..., None]), 0.0)
    new_exp = jnp.where(new_valid, jnp.exp(new_scores - local_peak[..., None]), 0.0)
    local_total = jnp.sum(suffix_exp, axis=-1) + jnp.sum(new_exp, axis=-1)
    local_out = jnp.einsum(
        "sqk,skx->sqx",
        suffix_exp.astype(jnp.bfloat16),
        suffix_latent,
        preferred_element_type=jnp.float32,
    ) + jnp.einsum(
        "sqk,skx->sqx", new_exp.astype(jnp.bfloat16), new_latent, preferred_element_type=jnp.float32
    )
    peak = jnp.maximum(prefix_peak, local_peak)
    prefix_factor = jnp.exp(prefix_peak - peak)
    local_factor = jnp.exp(local_peak - peak)
    merged = (prefix_factor[..., None] * prefix_out + local_factor[..., None] * local_out) / (
        prefix_factor * prefix_total + local_factor * local_total
    )[..., None]
    attended = merged.astype(jnp.bfloat16).reshape(row_count, 2, head_count, LAT)
    values = (
        jnp.einsum("sthl,hlv->sthv", attended, w_uv, preferred_element_type=jnp.float32)
        .astype(jnp.bfloat16)
        .reshape(row_count, 2, head_count * VDIM)
    )
    partial_sums = jnp.einsum(
        "stf,fd->std",
        lax.all_gather(values, "sample", axis=0, tiled=True),
        w_out,
        preferred_element_type=jnp.float32,
    )
    return lax.psum_scatter(partial_sums, "head", scatter_dimension=2, tiled=True).astype(
        jnp.bfloat16
    )


def solution(mesh):
    placed = (
        P(("prompt", "sample"), None, "head"),
        P(("prompt", "sample"), None, "head"),
        P(("prompt", "sample"), None, None),
        P(("prompt", "sample"), None, None),
        P(("prompt", "sample"), None, None),
        P(("prompt", "sample"), None, None),
        P(("prompt", "sample"), None, None),
        P(("prompt", "sample"), None, None),
        P(("prompt", "sample")),
        P(("prompt", "sample")),
        P("head", None, None),
        P("head", None, None),
        P("head", "sample"),
    )
    return jax.shard_map(
        shards,
        mesh=mesh,
        in_specs=placed,
        out_specs=P("prompt", None, ("sample", "head")),
        check_vma=False,
    )
```

profile of v0, /device:TPU:1, one launch (start us, length us, event | category | flops | bytes accessed | tf_op | source)
XLA Modules:
  0.0 209.3 jit_solution(18188056059113263734)
XLA Ops:
  6.5 1.1 reshape.157
  7.6 1.0 convolution_convert_fusion.1
  8.6 0.2 copy.95
  8.8 0.8 reshape.204
  9.6 12.0 %all-to-all-start.1 = ((bf16[32,2,768]{2,1,0:T(2,128)(2,1)}), bf16[32,2,768]{2,1,0:T(2,128)(2,1)S(1)}, u32[]{:S(2)}, u32[]{:S(2)}) async-start(bf16[32,2,768]{2,1,0:T(2,128)(2,1)} %reshape.204), calls=%async_computation.1 | async-start | bytes 196608 | tf_op jit(solution)/shard_map/all_to_all | solution.py:61
  21.6 0.9 reshape.155
  22.6 1.7 fusion.20
  24.3 0.5 convolution_convert_fusion
  24.8 1.7 copy.63
  26.5 4.3 %all-to-all-done.1 = bf16[32,2,768]{2,1,0:T(2,128)(2,1)S(1)} async-done(((bf16[32,2,768]{2,1,0:T(2,128)(2,1)}), bf16[32,2,768]{2,1,0:T(2,128)(2,1)S(1)}, u32[]{:S(2)}, u32[]{:S(2)}) %all-to-all-start.1) | async-done | bytes 98336 | tf_op jit(solution)/shard_map/all_to_all | solution.py:61
  30.8 5.1 %all-to-all-start = ((bf16[32,2,12,512]{3,1,2,0:T(2,128)(2,1)}), bf16[32,2,12,512]{3,1,2,0:T(2,128)(2,1)}, u32[]{:S(2)}, u32[]{:S(2)}) async-start(bf16[32,2,12,512]{3,1,2,0:T(2,128)(2,1)} %copy.63), calls=%async_computation | async-start | bytes 1572864 | tf_op jit(solution)/shard_map/all_to_all | solution.py:55
  35.8 0.2 reshape.205
  36.1 0.8 reshape.158
  36.8 19.6 %all-to-all-done = bf16[32,2,12,512]{3,1,2,0:T(2,128)(2,1)} async-done(((bf16[32,2,12,512]{3,1,2,0:T(2,128)(2,1)}), bf16[32,2,12,512]{3,1,2,0:T(2,128)(2,1)}, u32[]{:S(2)}, u32[]{:S(2)}) %all-to-all-start) | async-done | bytes 786464 | tf_op jit(solution)/shard_map/all_to_all | solution.py:55
  56.5 1.3 copy.64
  57.8 1.1 reshape.156
  58.9 3.0 %fusion.7 = f32[768,2048]{1,0:T(8,128)S(1)} fusion(bf16[768,512]{1,0:T(8,128)(2,1)} %reshape.156, bf16[1,2048,512]{2,1,0:T(8,128)(2,1)S(1)} %copy-done), kind=kOutput, calls=%fused_computation.12 | convolution fusion | flops 1610612736 | bytes 9175040 | tf_op jit(solution)/shard_map/rx,kx->rk/dot_general | solution.py:65
  61.9 1.1 fusion.56
  63.0 2.6 %fusion = (f32[768]{0:T(1024)S(1)}, bf16[768,2048]{1,0:T(8,128)(2,1)}) fusion(f32[768,2048]{1,0:T(8,128)S(1)} %get-tuple-element.18, f32[768]{0:T(1024)S(1)} %get-tuple-element.17), kind=kLoop, calls=%fused_computation.5 | loop fusion | flops 4717824 | bytes 9443328 | tf_op jit(solution)/shard_map/reduce_sum | solution.py:70
  65.6 0.7 reshape.162
  66.3 6.3 %all-to-all-start.4 = ((f32[32,2,12]{2,1,0:T(2,128)}), f32[32,2,12]{2,1,0:T(2,128)S(1)}, u32[]{:S(2)}, u32[]{:S(2)}) async-start(f32[32,2,12]{2,1,0:T(2,128)} %reshape.162), calls=%async_computation.4 | async-start | bytes 65536 | tf_op jit(solution)/shard_map/all_to_all | solution.py:97
  73.0 0.7 reshape.159
  73.7 6.1 %dot_general.53 = bf16[32,2,12,2048]{3,2,1,0:T(8,128)(2,1)} reshape(bf16[768,2048]{1,0:T(8,128)(2,1)} %get-tuple-element.10) | data formatting | bytes 6291456 | tf_op jit(solution)/shard_map/dot_general | solution.py:71
  79.8 1.5 all-to-all-done.4
  81.3 7.9 %all-to-all-start.2 = ((f32[32,2,12]{2,1,0:T(2,128)}), f32[32,2,12]{2,1,0:T(2,128)S(1)}, u32[]{:S(2)}, u32[]{:S(2)}) async-start(f32[32,2,12]{2,1,0:T(2,128)} %reshape.159), calls=%async_computation.2 | async-start | bytes 65536 | tf_op jit(solution)/shard_map/all_to_all | solution.py:86
  89.2 4.1 %fusion.4 = f32[32,2,12,512]{3,0,2,1:T(8,128)S(1)} fusion(bf16[32,2,12,2048]{3,2,1,0:T(8,128)(2,1)} %dot_general.53, bf16[1,2048,512]{2,1,0:T(8,128)(2,1)S(1)} %copy-done), kind=kOutput, calls=%fused_computation.9 | convolution fusion | flops 1610612736 | bytes 6815744 | tf_op jit(solution)/shard_map/dot_general | solution.py:71
  93.3 2.4 %copy.70 = f32[32,2,12,512]{3,1,2,0:T(2,128)} copy(f32[32,2,12,512]{3,0,2,1:T(8,128)S(1)} %fusion.4) | data formatting | bytes 3145728 | tf_op jit(solution)/shard_map/dot_general | solution.py:71
  95.7 2.0 all-to-all-done.2
  97.7 7.3 %all-to-all-start.3 = ((f32[32,2,12,512]{3,1,2,0:T(2,128)}), f32[32,2,12,512]{3,1,2,0:T(2,128)}, u32[]{:S(2)}, u32[]{:S(2)}) async-start(f32[32,2,12,512]{3,1,2,0:T(2,128)} %copy.70), calls=%async_computation.3 | async-start | bytes 3145728 | tf_op jit(solution)/shard_map/all_to_all | solution.py:75
  105.2 0.2 fusion.58
  105.4 0.2 select_reduce_fusion.1
  105.6 1.9 fusion.57
  107.5 0.3 select_reduce_fusion
  107.8 0.2 fusion.35
  108.1 1.2 fusion.39
  109.3 0.6 gather_fusion.2
  109.9 0.6 gather_fusion.1
  110.7 29.2 %all-to-all-done.3 = f32[32,2,12,512]{3,1,2,0:T(2,128)} async-done(((f32[32,2,12,512]{3,1,2,0:T(2,128)}), f32[32,2,12,512]{3,1,2,0:T(2,128)}, u32[]{:S(2)}, u32[]{:S(2)}) %all-to-all-start.3) | async-done | bytes 1572896 | tf_op jit(solution)/shard_map/all_to_all | solution.py:75
  139.9 2.6 %gather_fusion = f32[12,2,12,512]{3,1,2,0:T(2,128)S(1)} fusion(f32[32,2,12,512]{3,1,2,0:T(2,128)} %all-to-all-done.3, s32[1024]{0:T(1024)S(1)} %pad_clamp_fusion), kind=kCustom, calls=%fused_computation.2 | custom fusion | bytes 1179696 | tf_op jit(solution)/shard_map/jit(_take)/gather | solution.py:74
  142.7 1.4 fusion.19
  144.2 1.8 fusion.27
  146.2 11.4 %all_gather.3 = bf16[48,2,1536]{2,1,0:T(2,128)(2,1)S(1)} all-gather(bf16[12,2,1536]{2,1,0:T(2,128)(2,1)S(1)} %reshape.165), channel_id=1, replica_groups=mesh['prompt'=8,'sample'=4,'head'=8] {'sample'}, dimensions={0}, use_global_device_ids=true | all-gather | bytes 368640 | tf_op jit(solution)/shard_map/all_gather | solution.py:151
  157.6 3.6 %fusion.2 = f32[48,2,1792]{2,0,1:T(8,128)S(1)} fusion(bf16[1536,1792]{1,0:T(8,128)(2,1)} %param.27, bf16[48,2,1536]{2,1,0:T(2,128)(2,1)S(1)} %all_gather.3), kind=kOutput, calls=%fused_computation.7 | convolution fusion | flops 528482304 | bytes 6488064 | tf_op jit(solution)/shard_map/stf,fd->std/dot_general | solution.py:149
  161.2 2.2 %copy.80 = f32[48,2,1792]{0,1,2:T(2,128)} copy(f32[48,2,1792]{2,0,1:T(8,128)S(1)} %fusion.2) | data formatting | bytes 1376256
  163.4 3.2 %reshape.202 = f32[1792,96]{1,0:T(8,128)} reshape(f32[1792,2,48]{2,1,0:T(2,128)} %bitcast.64) | data formatting | bytes 1376256
  166.6 34.1 %reduce-scatter.4.cloned.1.call-done = f32[224,96]{1,0:T(8,128)} async-done(((f32[1792,96]{1,0:T(8,128)}), f32[224,96]{1,0:T(8,128)}) %reduce-scatter.4.cloned.1.call-update) | async-done | bytes 86032
  200.7 1.0 reshape.203
  201.8 0.7 copy.75
  (46 shorter events, 1.3 us)
Async XLA Ops:
  6.5 52.3 %copy-start = (bf16[1,2048,512]{2,1,0:T(8,128)(2,1)S(1)}, bf16[1,2048,512]{2,1,0:T(8,128)(2,1)}, u32[]{:S(2)}) copy-start(bf16[1,2048,512]{2,1,0:T(8,128)(2,1)} %param.19) | copy-start | bytes 6291460
  6.5 17.8 %copy-start.6 = (s32[12]{0:T(128)S(1)}, s32[12]{0:T(128)}, u32[]{:S(2)}) copy-start(s32[12]{0:T(128)} %param.23) | copy-start | bytes 148
  9.6 21.2 %all-to-all-start.1 = ((bf16[32,2,768]{2,1,0:T(2,128)(2,1)}), bf16[32,2,768]{2,1,0:T(2,128)(2,1)S(1)}, u32[]{:S(2)}, u32[]{:S(2)}) async-start(bf16[32,2,768]{2,1,0:T(2,128)(2,1)} %reshape.204), calls=%async_computation.1 | async-start | bytes 196608 | tf_op jit(solution)/shard_map/all_to_all | solution.py:61
  30.8 25.7 %all-to-all-start = ((bf16[32,2,12,512]{3,1,2,0:T(2,128)(2,1)}), bf16[32,2,12,512]{3,1,2,0:T(2,128)(2,1)}, u32[]{:S(2)}, u32[]{:S(2)}) async-start(bf16[32,2,12,512]{3,1,2,0:T(2,128)(2,1)} %copy.63), calls=%async_computation | async-start | bytes 1572864 | tf_op jit(solution)/shard_map/all_to_all | solution.py:55
  58.9 3.0 %copy-start.2 = (bf16[768,64]{1,0:T(8,128)(2,1)S(1)}, bf16[768,64]{1,0:T(8,128)(2,1)}, u32[]{:S(2)}) copy-start(bf16[768,64]{1,0:T(8,128)(2,1)} %reshape.158) | copy-start | bytes 294916
  58.9 3.0 %copy-start.3 = (bf16[1,64,2048]{2,1,0:T(8,128)(2,1)S(1)}, bf16[1,64,2048]{2,1,0:T(8,128)(2,1)}, u32[]{:S(2)}) copy-start(bf16[1,64,2048]{2,1,0:T(8,128)(2,1)} %param.20) | copy-start | bytes 786436
  63.0 9.8 %copy-start.5 = (bf16[12,2,768]{2,1,0:T(2,128)(2,1)S(1)}, bf16[12,2,768]{2,1,0:T(2,128)(2,1)}, u32[]{:S(2)}) copy-start(bf16[12,2,768]{2,1,0:T(2,128)(2,1)} %param.16) | copy-start | bytes 110596
  66.3 15.0 %all-to-all-start.4 = ((f32[32,2,12]{2,1,0:T(2,128)}), f32[32,2,12]{2,1,0:T(2,128)S(1)}, u32[]{:S(2)}, u32[]{:S(2)}) async-start(f32[32,2,12]{2,1,0:T(2,128)} %reshape.162), calls=%async_computation.4 | async-start | bytes 65536 | tf_op jit(solution)/shard_map/all_to_all | solution.py:97
  81.3 16.4 %all-to-all-start.2 = ((f32[32,2,12]{2,1,0:T(2,128)}), f32[32,2,12]{2,1,0:T(2,128)S(1)}, u32[]{:S(2)}, u32[]{:S(2)}) async-start(f32[32,2,12]{2,1,0:T(2,128)} %reshape.159), calls=%async_computation.2 | async-start | bytes 65536 | tf_op jit(solution)/shard_map/all_to_all | solution.py:86
  95.7 9.4 %copy-start.7 = (s32[12]{0:T(128)S(1)}, s32[12]{0:T(128)}, u32[]{:S(2)}) copy-start(s32[12]{0:T(128)} %param.24) | copy-start | bytes 148
  95.7 9.5 %copy-start.8 = (bf16[12,2,512]{2,1,0:T(2,128)(2,1)S(1)}, bf16[12,2,512]{2,1,0:T(2,128)(2,1)}, u32[]{:S(2)}) copy-start(bf16[12,2,512]{2,1,0:T(2,128)(2,1)} %param.17) | copy-start | bytes 73732
  95.7 9.7 %copy-start.10 = (bf16[12,2,64]{2,1,0:T(2,128)(2,1)S(1)}, bf16[12,2,64]{2,1,0:T(2,128)(2,1)}, u32[]{:S(2)}) copy-start(bf16[12,2,64]{2,1,0:T(2,128)(2,1)} %param.18) | copy-start | bytes 9220
  95.7 11.8 %copy-start.4 = (bf16[12,64,128]{2,1,0:T(8,128)(2,1)S(1)}, bf16[12,64,128]{2,1,0:T(8,128)(2,1)}, u32[]{:S(2)}) copy-start(bf16[12,64,128]{2,1,0:T(8,128)(2,1)} %param.22) | copy-start | bytes 589828
  97.7 42.2 %all-to-all-start.3 = ((f32[32,2,12,512]{3,1,2,0:T(2,128)}), f32[32,2,12,512]{3,1,2,0:T(2,128)}, u32[]{:S(2)}, u32[]{:S(2)}) async-start(f32[32,2,12,512]{3,1,2,0:T(2,128)} %copy.70), calls=%async_computation.3 | async-start | bytes 3145728 | tf_op jit(solution)/shard_map/all_to_all | solution.py:75
  105.0 95.6 %reduce-scatter.4.cloned.1.call-start = ((), (), s32[]{:S(2)}) async-start(), calls=%async_computation.6 | async-start | bytes 1032192
  105.1 3.0 %copy-start.1 = (bf16[12,128,512]{2,1,0:T(8,128)(2,1)S(1)}, bf16[12,128,512]{2,1,0:T(8,128)(2,1)}, u32[]{:S(2)}) copy-start(bf16[12,128,512]{2,1,0:T(8,128)(2,1)} %param.21) | copy-start | bytes 4718596
  110.7 32.0 %copy-start.9 = (bf16[12,2,512]{2,1,0:T(2,128)(2,1)S(1)}, bf16[12,2,512]{2,1,0:T(2,128)(2,1)}, u32[]{:S(2)}) copy-start(bf16[12,2,512]{2,1,0:T(2,128)(2,1)} %param.17) | copy-start | bytes 73732
Sparse Core Ops, SparseCore 0:
  166.7 33.8 reduce-scatter.3
where the time goes:
time: 212 us; the launch traced here: 209 us
  waiting for transfers between devices  90.7 us (43%)
  starting transfers between devices  38.6 us (18%)
  local copies, waits for them, and re-layouts  29.7 us (14%)
  matrix products  22 us (10%)
  between operations  13.8 us (7%)
  blocking collectives  11.4 us (5%)
  other arithmetic  3.08 us (1%)
    unnamed x2, waiting for transfers between devices  34.1 us
    all_to_all x1, waiting for transfers between devices, shards(): lax.all_to_all(weighted.reshape(slot_count, item_count, head_count, LAT),...  29.2 us
    all_to_all x1, waiting for transfers between devices, shards(): lax.all_to_all(lead_send, ('prompt', 'sample'), split_axis=0, concat_axis...  19.6 us
    all_to_all x1, starting transfers between devices, shards(): lax.all_to_all(rope_send, ('prompt', 'sample'), split_axis=0, concat_axis...  12 us
    all_gather x1, blocking collectives, shards(): lax.all_gather(values, 'sample', axis=0, tiled=True)  11.4 us
    dot_general x2, local copies, waits for them, and re-layouts, shards(): jnp.dot(expo_vals.astype(jnp.bfloat16), cache_latent, preferred_element_t...  8.42 us
    all_to_all x1, starting transfers between devices, shards(): lax.all_to_all(row_peak.reshape(slot_count, item_count, head_count), ('pr...  7.87 us
    unnamed x28, local copies, waits for them, and re-layouts  7.52 us
  transfers between devices with their start and end apart: 6, of which 6 were waited for; matrix products, arithmetic and copies ran while one was open for 12% of the time, Pallas kernels for 0%

commit v1 on v0

v1 whole, which is shorter than its diff:
```python
import functools
import math

import jax
import jax.numpy as jnp
from jax import lax
from jax.experimental import pallas as pl
from jax.experimental.pallas import tpu as pltpu
from jax.sharding import PartitionSpec as P

NOPE = 128
ROPE = 64
LAT = 512
VDIM = 128
F32 = jnp.float32
BF16 = jnp.bfloat16
MESH = pl.DeviceIdType.MESH
FLOOR = -1e30
SCALE = 1.0 / math.sqrt(NOPE + ROPE)
EXP2_SCALE = SCALE * math.log2(math.e)
CHUNKS = 2
NT = (((1,), (1,)), ((), ()))


def dot(left, right):
    return jnp.dot(left, right, preferred_element_type=F32)


def dot_nt(left, right):
    return lax.dot_general(left, right, NT, preferred_element_type=F32)


def put(ref, first, count, stride, value):
    for tile in range(ref.shape[0]):
        ref[tile, pl.ds(first, count, stride=stride), :] = value[:, 128 * tile : 128 * (tile + 1)]


def take(ref, first, count, stride):
    tiles = [ref[tile, pl.ds(first, count, stride=stride), :] for tile in range(ref.shape[0])]
    return jnp.concatenate(tiles, axis=1)


def whole(ref, rows=slice(None)):
    return jnp.concatenate([ref[tile, rows, :] for tile in range(ref.shape[0])], axis=1)


def fill(ref, value, rows=slice(None)):
    for tile in range(ref.shape[0]):
        ref[tile, rows, :] = value[:, 128 * tile : 128 * (tile + 1)]


def iota(shape, axis):
    return lax.broadcasted_iota(jnp.int32, shape, axis)


def kernel(
    sizes,
    sp_ref,
    len_ref,
    q_ref,
    r_ref,
    nl_ref,
    nr_ref,
    plat_hbm,
    prope_hbm,
    slat_hbm,
    srope_hbm,
    wuk_hbm,
    wuv_hbm,
    wout_hbm,
    out_ref,
    plat,
    prope,
    slat,
    srope,
    wuk,
    wuv,
    wout,
    tok,
    ntok,
    qf,
    qb,
    sb,
    rb,
    xf,
    lqf,
    lrf,
    lsc,
    lof,
    lvf,
    lse_col,
    plf,
    prf,
    sc,
    pb,
    pof,
    rvf,
    back,
    rr,
    cf,
    vg,
    lhs,
    part,
    blocks,
    sums,
    load_sem,
    q_send,
    q_recv,
    b_send,
    b_recv,
    v_send,
    v_recv,
    o_send,
    o_recv,
):
    nz, ny, nh = sizes
    slots = nz * ny
    samples = q_ref.shape[0]
    pairs = 2 * samples
    heads = wuk.shape[0]
    wide = 2 * heads
    z = lax.axis_index("prompt")
    y = lax.axis_index("sample")
    head = lax.axis_index("head")
    here = z * ny + y

    loads = [
        pltpu.make_async_copy(source, target, load_sem.at[index])
        for index, (source, target) in enumerate(
            (
                (wuk_hbm, wuk),
                (slat_hbm, slat),
                (srope_hbm, srope),
                (wuv_hbm, wuv),
                (plat_hbm.at[0], plat),
                (prope_hbm.at[0], prope),
                (wout_hbm, wout),
            )
        )
    ]
    for load in loads:
        load.start()
    load_wuk, load_slat, load_srope, load_wuv, load_plat, load_prope, load_wout = loads

    def ahead(k):
        step = k // ny
        half = (step + 1) // 2
        shift = jnp.where(step % 2 == 1, half, nz - half)
        return lax.rem(z + shift, nz), lax.rem(y + k % ny, ny)

    def behind(k):
        step = k // ny
        half = (step + 1) // 2
        shift = jnp.where(step % 2 == 1, nz - half, half)
        return lax.rem(z + shift, nz), lax.rem(y + ny - k % ny, ny)

    barrier = pltpu.get_barrier_semaphore()

    @pl.loop(1, slots)
    def _(k):
        to_z, to_y = ahead(k)
        pl.semaphore_signal(
            barrier, inc=1, device_id={"prompt": to_z, "sample": to_y}, device_id_type=MESH
        )

    @pl.loop(1, nh)
    def _(d):
        pl.semaphore_signal(
            barrier, inc=1, device_id={"head": lax.rem(head + d, nh)}, device_id_type=MESH
        )

    for s in range(samples):
        tok[2 * s : 2 * s + 2, :] = q_ref[s].astype(F32)
        ntok[2 * s : 2 * s + 2, :LAT] = nl_ref[s].astype(F32)
        ntok[2 * s : 2 * s + 2, LAT:] = jnp.zeros((2, NOPE), F32)
        ntok[2 * s : 2 * s + 2, LAT : LAT + ROPE] = nr_ref[s].astype(F32)
    for h in range(heads):
        qf[pl.ds(h, pairs, stride=wide), :] = tok[:, h * NOPE : (h + 1) * NOPE]
    for s in range(samples):
        tok[2 * s : 2 * s + 2, : heads * ROPE] = r_ref[s].astype(F32)
    low = iota((pairs, NOPE), 1) < ROPE
    for h in range(heads):
        both = tok[:, h // 2 * NOPE : (h // 2 + 1) * NOPE]
        if h % 2 == 1:
            both = pltpu.roll(both, ROPE, 1)
        rope_rows = jnp.where(low, both, 0.0)
        qf[pl.ds(heads + h, pairs, stride=wide), :] = rope_rows
        lrf[pl.ds(h, pairs, stride=16), :] = rope_rows
    for h in range(heads, 16):
        lrf[pl.ds(h, pairs, stride=16), :] = jnp.zeros((pairs, NOPE), F32)
        put(lqf, h, pairs, 16, jnp.zeros((pairs, LAT), F32))
    for s in range(samples):
        qb[s] = qf[2 * wide * s : 2 * wide * (s + 1), :].astype(BF16)

    pl.semaphore_wait(barrier, slots - 1 + nh - 1)

    def query_copy(k):
        to_z, to_y = ahead(k)
        return pltpu.make_async_remote_copy(
            src_ref=sb.at[k],
            dst_ref=rb.at[k],
            send_sem=q_send.at[k],
            recv_sem=q_recv.at[k],
            device_id={"prompt": to_z, "sample": to_y},
            device_id_type=MESH,
        )

    def sample_for(owner):
        found = 0
        for s in range(samples):
            found = jnp.where(sp_ref[s] == owner, s, found)
        return found

    rb[0] = qb[sample_for(here)]

    @pl.loop(1, slots)
    def _(k):
        to_z, to_y = ahead(k)
        sb[k] = qb[sample_for(to_z * ny + to_y)]
        query_copy(k).start()

    load_wuk.wait()
    for h in range(heads):
        rows = qf[pl.ds(h, pairs, stride=wide), :].astype(BF16)
        put(lqf, h, pairs, 16, dot(rows, wuk[h]))
    load_slat.wait()
    load_srope.wait()
    lane = iota((32, 128), 1)
    for s in range(samples):
        rows = slice(32 * s, 32 * s + 32)
        part_scores = dot_nt(whole(lqf, rows).astype(BF16), slat[s]) + dot(
            lrf[rows, :].astype(BF16)[:, :ROPE], srope[s]
        )
        lsc[rows, :] = jnp.where(lane < len_ref[s], part_scores, FLOOR)
    new_latent = ntok[:, :LAT].astype(BF16)
    new_rope = ntok[:, LAT:].astype(BF16)
    count = 16 * pairs
    new_scores = dot_nt(whole(lqf).astype(BF16), new_latent) + dot_nt(
        lrf[...].astype(BF16), new_rope
    )
    row, key = iota((count, pairs), 0), iota((count, pairs), 1)
    valid = ((key >> 1) == (row >> 5)) & ((key & 1) <= ((row >> 4) & 1))
    new_scores = jnp.where(valid, new_scores, FLOOR)
    old_scores = lsc[...]
    peak = jnp.maximum(
        jnp.max(old_scores, axis=1, keepdims=True), jnp.max(new_scores, axis=1, keepdims=True)
    )
    old_exp = jnp.exp2((old_scores - peak) * EXP2_SCALE)
    new_exp = jnp.exp2((new_scores - peak) * EXP2_SCALE)
    total = jnp.sum(old_exp, axis=1, keepdims=True) + jnp.sum(new_exp, axis=1, keepdims=True)
    lse_col[...] = jnp.broadcast_to(peak * SCALE + jnp.log(total), lse_col.shape)
    lsc[...] = old_exp
    new_out = dot(new_exp.astype(BF16), new_latent)
    inverse = 1.0 / total
    for s in range(samples):
        rows = slice(32 * s, 32 * s + 32)
        own_out = new_out[rows] + dot(lsc[rows, :].astype(BF16), slat[s])
        fill(lof, own_out * inverse[rows], rows)
    load_wuv.wait()
    for h in range(heads):
        rows = take(lof, h, pairs, 16).astype(BF16)
        lvf[pl.ds(h, pairs, stride=16), :] = dot(rows, wuv[h])
    for h in range(heads, 16):
        lvf[pl.ds(h, pairs, stride=16), :] = jnp.zeros((pairs, VDIM), F32)

    load_plat.wait()
    load_prope.wait()
    size = slots // CHUNKS
    duo = 2 * size
    rows_all = wide * size
    for h in range(heads, 16):
        rvf[pl.ds(h, duo, stride=16), :] = jnp.zeros((duo, VDIM), F32)

    def back_copy(k):
        to_z, to_y = behind(k)
        return pltpu.make_async_remote_copy(
            src_ref=back.at[k],
            dst_ref=rr.at[here],
            send_sem=b_send.at[k],
            recv_sem=b_recv.at[k],
            device_id={"prompt": to_z, "sample": to_y},
            device_id_type=MESH,
        )

    @pl.loop(0, CHUNKS)
    def _(chunk):
        base = chunk * size

        @pl.loop(0, size)
        def _(i):
            @pl.when(base + i > 0)
            def _():
                query_copy(base + i).wait_recv()

        xf[...] = rb[pl.ds(base, size)].astype(F32).reshape(xf.shape)
        for h in range(heads):
            rows = xf[pl.ds(h, duo, stride=wide), :].astype(BF16)
            put(plf, h, duo, heads, dot(rows, wuk[h]))
            prf[pl.ds(h, duo, stride=heads), :] = xf[pl.ds(heads + h, duo, stride=wide), :]
        lat_rows = whole(plf).astype(BF16)
        rope_rows = prf[...].astype(BF16)[:, :ROPE]
        length = plat.shape[0]
        tile = min(512, length)
        peak = None
        for at in range(0, length, tile):
            scores = dot_nt(lat_rows, plat[at : at + tile, :]) + dot(
                rope_rows, prope[:, at : at + tile]
            )
            sc[:, at : at + tile] = scores
            top = jnp.max(scores, axis=1, keepdims=True)
            peak = top if peak is None else jnp.maximum(peak, top)
        total = jnp.zeros_like(peak)
        for at in range(0, length, tile):
            probs = jnp.exp2((sc[:, at : at + tile] - peak) * EXP2_SCALE)
            total = total + jnp.sum(probs, axis=1, keepdims=True)
            pb[:, at : at + tile] = probs.astype(BF16)
        fill(pof, dot(pb[...], plat[...]) * (1.0 / total))
        for h in range(heads):
            rows = take(pof, h, duo, heads).astype(BF16)
            rvf[pl.ds(h, duo, stride=16), :] = dot(rows, wuv[h])
        lse = peak * SCALE + jnp.log(total)
        first = lse.astype(BF16).astype(F32)
        second = (lse - first).astype(BF16).astype(F32)
        third = lse - first - second
        row, lane = iota((rows_all, 128), 0), iota((rows_all, 128), 1)
        place = row - heads * ((row * 43691) >> 19)
        spread = (
            jnp.where(lane == place, first, 0.0)
            + jnp.where(lane == place + 16, second, 0.0)
            + jnp.where(lane == place + 32, third, 0.0)
        ).astype(BF16)
        at, of = iota((duo, rows_all), 0) * heads, iota((duo, rows_all), 1)
        pick = jnp.where((of >= at) & (of < at + heads), 1.0, 0.0).astype(BF16)
        rvf[pl.ds(heads, duo, stride=16), :] = dot(pick, spread)
        back[pl.ds(base, size)] = rvf[...].reshape(size, 32, VDIM).astype(BF16)

        @pl.loop(0, size)
        def _(i):
            @pl.when(base + i > 0)
            def _():
                back_copy(base + i).start()

    rr[here] = back[0]

    @pl.loop(1, slots)
    def _(k):
        back_copy(k).wait_recv()

    for s in range(samples):
        cf[32 * s : 32 * s + 32, :] = rr[sp_ref[s]].astype(F32)
    row, lane = iota((16, 128), 0), iota((16, 128), 1)
    mine = (lane == row) | (lane == row + 16) | (lane == row + 32)
    for pair in range(pairs):
        rows = slice(16 * pair, 16 * pair + 16)
        stat = jnp.broadcast_to(cf[16 * pair + heads : 16 * pair + heads + 1, :], (16, 128))
        lse_prompt = jnp.sum(jnp.where(mine, stat, 0.0), axis=1, keepdims=True)
        lse_local = lse_col[rows, :]
        top = jnp.maximum(lse_prompt, lse_local)
        weight_prompt = jnp.exp(lse_prompt - top)
        weight_local = jnp.exp(lse_local - top)
        lvf[rows, :] = (weight_prompt * cf[rows, :] + weight_local * lvf[rows, :]) / (
            weight_prompt + weight_local
        )
    half = heads // 2
    columns = [
        jnp.concatenate(
            [lvf[pl.ds(h, pairs, stride=16), :], lvf[pl.ds(h + half, pairs, stride=16), :]], axis=0
        )
        for h in range(half)
    ]
    vg[y] = jnp.concatenate(columns, axis=1).astype(BF16)

    def value_copy(d):
        return pltpu.make_async_remote_copy(
            src_ref=vg.at[y],
            dst_ref=vg.at[y],
            send_sem=v_send.at[d],
            recv_sem=v_recv.at[d],
            device_id={"sample": lax.rem(y + d, ny)},
            device_id_type=MESH,
        )

    for d in range(1, ny):
        value_copy(d).start()
    load_wout.wait()
    for d in range(1, ny):
        value_copy(d).wait_recv()

    for d in range(ny):
        gathered = vg[d].astype(F32)
        lhs[pairs * d : pairs * (d + 1), : half * VDIM] = gathered[:pairs]
        lhs[pairs * d : pairs * (d + 1), half * VDIM :] = gathered[pairs:]
    left = lhs[...].astype(BF16)
    columns_all = wout.shape[1]
    width = columns_all // nh

    def sum_copy(j):
        return pltpu.make_async_remote_copy(
            src_ref=blocks.at[j],
            dst_ref=sums.at[head],
            send_sem=o_send.at[j],
            recv_sem=o_recv.at[head],
            device_id={"head": j},
            device_id_type=MESH,
        )

    done = 0
    tile = 256
    for at in range(0, columns_all, tile):
        stop = min(at + tile, columns_all)
        part[:, at:stop] = dot(left, wout[:, at:stop])
        while done < nh and (done + 1) * width <= stop:
            start = done * width
            floor = start // 128 * 128
            ceil = -(-(start + width) // 128) * 128
            block = part[:, floor:ceil]
            if start > floor:
                block = pltpu.roll(block, ceil - start, 1)
            blocks[done] = block[:, :width].astype(BF16)

            @pl.when(head != done)
            def _(j=done):
                sum_copy(j).start()

            done += 1
    result = blocks[head].astype(F32)
    for d in range(1, nh):
        source = lax.rem(head + d, nh)
        pltpu.make_async_remote_copy(
            src_ref=blocks.at[source],
            dst_ref=sums.at[source],
            send_sem=o_send.at[source],
            recv_sem=o_recv.at[source],
            device_id={"head": source},
            device_id_type=MESH,
        ).wait_recv()
        result = result + sums[source].astype(F32)
    out_ref[...] = result.astype(BF16)

    @pl.loop(1, slots)
    def _(k):
        query_copy(k).wait_send()
        back_copy(k).wait_send()

    for d in range(1, ny):
        value_copy(d).wait_send()

    @pl.loop(1, nh)
    def _(d):
        sum_copy(lax.rem(head + d, nh)).wait_send()


def shards(
    q_nope,
    q_rope,
    new_latent,
    new_rope,
    prompt_latent,
    prompt_rope,
    suffix_latent,
    suffix_rope,
    sample_prompt,
    suffix_len,
    w_uk,
    w_uv,
    w_out,
):
    nz, ny, nh = (lax.axis_size(name) for name in ("prompt", "sample", "head"))
    slots = nz * ny
    samples = q_nope.shape[0]
    pairs = 2 * samples
    heads = w_uk.shape[0]
    length = prompt_latent.shape[1]
    width = w_out.shape[1] // nh
    size = slots // CHUNKS
    duo = 2 * size
    rows_all = 2 * heads * size
    count = 16 * pairs
    vmem = pltpu.VMEM
    dma = pltpu.SemaphoreType.DMA
    in_vmem = pl.BlockSpec(memory_space=pltpu.VMEM)
    in_smem = pl.BlockSpec(memory_space=pltpu.SMEM)
    in_hbm = pl.BlockSpec(memory_space=pl.ANY)
    result = pl.pallas_call(
        functools.partial(kernel, (nz, ny, nh)),
        out_shape=jax.ShapeDtypeStruct((pairs * ny, width), BF16),
        in_specs=[in_smem] * 2 + [in_vmem] * 4 + [in_hbm] * 7,
        out_specs=in_vmem,
        scratch_shapes=[
            vmem(prompt_latent.shape[1:], BF16),
            vmem(prompt_rope.shape[1:], BF16),
            vmem(suffix_latent.shape, BF16),
            vmem(suffix_rope.shape, BF16),
            vmem(w_uk.shape, BF16),
            vmem(w_uv.shape, BF16),
            vmem(w_out.shape, BF16),
            vmem((pairs, heads * NOPE), F32),
            vmem((pairs, LAT + NOPE), F32),
            vmem((pairs * 2 * heads, NOPE), F32),
            vmem((samples, 4 * heads, NOPE), BF16),
            vmem((slots, 4 * heads, NOPE), BF16),
            vmem((slots, 4 * heads, NOPE), BF16),
            vmem((size * 4 * heads, NOPE), F32),
            vmem((LAT // 128, count, 128), F32),
            vmem((count, NOPE), F32),
            vmem((count, suffix_latent.shape[1]), F32),
            vmem((LAT // 128, count, 128), F32),
            vmem((count, VDIM), F32),
            vmem((count, VDIM), F32),
            vmem((LAT // 128, rows_all, 128), F32),
            vmem((rows_all, NOPE), F32),
            vmem((rows_all, length), F32),
            vmem((rows_all, length), BF16),
            vmem((LAT // 128, rows_all, 128), F32),
            vmem((16 * duo, VDIM), F32),
            vmem((slots, 32, VDIM), BF16),
            vmem((slots, 32, VDIM), BF16),
            vmem((count, VDIM), F32),
            vmem((ny, 2 * pairs, heads * VDIM // 2), BF16),
            vmem((ny * pairs, heads * VDIM), F32),
            vmem((ny * pairs, w_out.shape[1]), F32),
            vmem((nh, ny * pairs, width), BF16),
            vmem((nh, ny * pairs, width), BF16),
            dma((7,)),
            dma((slots,)),
            dma((slots,)),
            dma((slots,)),
            dma((slots,)),
            dma((ny,)),
            dma((ny,)),
            dma((nh,)),
            dma((nh,)),
        ],
        compiler_params=pltpu.CompilerParams(
            collective_id=0, has_side_effects=True, vmem_limit_bytes=56 * 1024 * 1024
        ),
        cost_estimate=pl.CostEstimate(
            flops=5 * 10**9, bytes_accessed=13 * 10**6, transcendentals=2 * 10**6
        ),
    )(
        sample_prompt,
        suffix_len,
        q_nope,
        q_rope,
        new_latent,
        new_rope,
        prompt_latent,
        prompt_rope,
        suffix_latent,
        suffix_rope,
        w_uk,
        w_uv,
        w_out,
    )
    return result.reshape(ny * samples, 2, width)


def solution(mesh):
    placed = (
        P(("prompt", "sample"), None, "head"),
        P(("prompt", "sample"), None, "head"),
        P(("prompt", "sample"), None, None),
        P(("prompt", "sample"), None, None),
        P(("prompt", "sample"), None, None),
        P(("prompt", "sample"), None, None),
        P(("prompt", "sample"), None, None),
        P(("prompt", "sample"), None, None),
        P(("prompt", "sample")),
        P(("prompt", "sample")),
        P("head", None, None),
        P("head", None, None),
        P("head", "sample"),
    )
    return jax.shard_map(
        shards,
        mesh=mesh,
        in_specs=placed,
        out_specs=P("prompt", None, ("sample", "head")),
        check_vma=False,
    )
```

time: 212 us -> 52 us (0.25)
  waiting for transfers between devices: 90.7 us -> 0 us
  Pallas kernels: 0 us -> 49.8 us
  starting transfers between devices: 38.6 us -> 0 us
  local copies, waits for them, and re-layouts: 29.7 us -> 1.45 us
  matrix products: 22 us -> 0 us
  between operations: 13.8 us -> 0.01 us
  blocking collectives: 11.4 us -> 0 us
  other arithmetic: 3.08 us -> 0 us
    all_to_all x5 -> x0, waiting for transfers between devices: 56.6 us -> none  [the longest x1 29.2 us: shards(): lax.all_to_all(weighted.reshape(slot_count, item_count, head_count, LAT),...]
    pallas_call x0 -> x1, Pallas kernels: none -> 49.8 us  [shards(): pl.pallas_call(functools.partial(kernel, (nz, ny, nh)), out_shape=jax.Sha...]
    all_to_all x5 -> x0, starting transfers between devices: 38.5 us -> none  [the longest x1 12 us: shards(): lax.all_to_all(rope_send, ('prompt', 'sample'), split_axis=0, concat_axis...]
    unnamed x2 -> x0, waiting for transfers between devices: 34.1 us -> none
    dot_general x14 -> x0, matrix products: 22 us -> none  [the longest x1 4.12 us: shards(): jnp.dot(expo_vals.astype(jnp.bfloat16), cache_latent, preferred_element_t...]
    all_gather x1 -> x0, blocking collectives: 11.4 us -> none  [shards(): lax.all_gather(values, 'sample', axis=0, tiled=True)]
    dot_general x2 -> x0, local copies, waits for them, and re-layouts: 8.42 us -> none  [shards(): jnp.dot(expo_vals.astype(jnp.bfloat16), cache_latent, preferred_element_t...]
    unnamed x28 -> x0, local copies, waits for them, and re-layouts: 7.52 us -> none
  transfers between devices with their start and end apart: 6 -> 0, of which waited for: 6 -> 0; matrix products, arithmetic and copies ran while one was open for 12% -> 0% of each run, Pallas kernels for 0% -> 0%
where the time goes in v1:
time: 52 us; the launch traced here: 51.3 us
  Pallas kernels  49.8 us (96%)
  local copies, waits for them, and re-layouts  1.45 us (3%)
    pallas_call x1, Pallas kernels, shards(): pl.pallas_call(functools.partial(kernel, (nz, ny, nh)), out_shape=jax.Sha...  49.8 us
    reshape x1, local copies, waits for them, and re-layouts, shards(): return result.reshape(ny * samples, 2, width)  1.45 us

profile of v1, /device:TPU:1, one launch (start us, length us, event | category | flops | bytes accessed | tf_op | source)
XLA Modules:
  0.0 51.3 jit_solution(18318422155962549022)
XLA Ops:
  0.0 49.8 %shard_map.127 = bf16[96,224]{1,0:T(8,128)(2,1)} custom-call(s32[12]{0:T(128)} %sp_ref.1, s32[12]{0:T(128)} %len_ref.1, bf16[12,2,1536]{2,1,0:T(2,128)(2,1)} %q_ref.1, bf16[12,2,768]{2,1,0:T(2,128)(2,1)} %r_ref.1, bf16[12,2,512]{2,1,0:T(2,128)(2,1)} %nl_ref.1, bf16[12,2,64]{2,1,0:T(2,128)(2,1)} %nr_ref.1, bf16[1,2048,512]{2,1,0:T(8,128)(2,1)} %plat_hbm.1, ...), custom_call_target="tpu_custom_call" | custom-call | flops 5000000000 | bytes 13000000 | tf_op jit(solution)/shard_map/pallas_call | solution.py:484
  49.8 1.5 %reshape.3 = bf16[48,2,224]{2,1,0:T(2,128)(2,1)} reshape(bf16[96,224]{1,0:T(8,128)(2,1)} %shard_map.127) | data formatting | bytes 86016 | tf_op jit(solution)/shard_map/reshape | solution.py:555

commit v2 on v1

v2 whole, which is shorter than its diff:
```python
import functools
import math

import jax
import jax.numpy as jnp
from jax import lax
from jax.experimental import pallas as pl
from jax.experimental.pallas import tpu as pltpu
from jax.sharding import PartitionSpec as P

NOPE = 128
ROPE = 64
LAT = 512
VDIM = 128
F32 = jnp.float32
BF16 = jnp.bfloat16
MESH = pl.DeviceIdType.MESH
FLOOR = -1e30
SCALE = 1.0 / math.sqrt(NOPE + ROPE)
EXP2_SCALE = SCALE * math.log2(math.e)
MOST = 16
NT = (((1,), (1,)), ((), ()))


def dot(left, right):
    return jnp.dot(left, right, preferred_element_type=F32)


def dot_nt(left, right):
    return lax.dot_general(left, right, NT, preferred_element_type=F32)


def put(ref, first, count, stride, value):
    for tile in range(ref.shape[0]):
        ref[tile, pl.ds(first, count, stride=stride), :] = value[:, 128 * tile : 128 * (tile + 1)]


def take(ref, first, count, stride):
    tiles = [ref[tile, pl.ds(first, count, stride=stride), :] for tile in range(ref.shape[0])]
    return jnp.concatenate(tiles, axis=1)


def whole(ref, rows=slice(None)):
    return jnp.concatenate([ref[tile, rows, :] for tile in range(ref.shape[0])], axis=1)


def fill(ref, value, rows=slice(None)):
    for tile in range(ref.shape[0]):
        ref[tile, rows, :] = value[:, 128 * tile : 128 * (tile + 1)]


def iota(shape, axis):
    return lax.broadcasted_iota(jnp.int32, shape, axis)


def kernel(
    sizes,
    sp_ref,
    len_ref,
    q_ref,
    r_ref,
    nl_ref,
    nr_ref,
    plat_hbm,
    prope_hbm,
    slat_hbm,
    srope_hbm,
    wuk_hbm,
    wuv_hbm,
    wout_hbm,
    out_ref,
    plat,
    prope,
    slat,
    srope,
    wuk,
    wuv,
    wout,
    tok,
    ntok,
    qf,
    qb,
    sb,
    rb,
    xf,
    lqf,
    lrf,
    lsc,
    lof,
    lvf,
    lse_col,
    plf,
    prf,
    sc,
    pb,
    pof,
    rvf,
    back,
    rr0,
    rr1,
    cf,
    vg,
    lhs,
    part,
    blocks,
    sums,
    final,
    load_sem,
    q_send,
    q_recv,
    b_send,
    b_recv,
    v_send,
    v_recv,
    o_send,
    o_recv,
):
    nz, ny, nh = sizes
    slots = nz * ny
    samples = q_ref.shape[0]
    pairs = 2 * samples
    heads = wuk.shape[0]
    half = heads // 2
    wide = 2 * heads
    spots = 2 * slots
    used = 2 * min(MOST, slots)
    z = lax.axis_index("prompt")
    y = lax.axis_index("sample")
    head = lax.axis_index("head")
    here = z * ny + y
    z_at = [lax.rem(z + d, nz) for d in range(nz)]
    y_at = [lax.rem(y + d, ny) for d in range(ny)]
    head_at = [lax.rem(head + d, nh) for d in range(nh)]

    def ahead(k):
        step = k // ny
        away = (step + 1) // 2
        return z_at[away if step % 2 == 1 else (nz - away) % nz], y_at[k % ny]

    def behind(k):
        step = k // ny
        away = (step + 1) // 2
        return z_at[(nz - away) % nz if step % 2 == 1 else away], y_at[(ny - k % ny) % ny]

    barrier = pltpu.get_barrier_semaphore()
    for k in range(1, slots):
        to_z, to_y = ahead(k)
        pl.semaphore_signal(
            barrier, inc=1, device_id={"prompt": to_z, "sample": to_y}, device_id_type=MESH
        )
    for d in range(1, nh):
        pl.semaphore_signal(
            barrier, inc=1, device_id={"head": head_at[d]}, device_id_type=MESH
        )

    loads = [
        pltpu.make_async_copy(source, target, load_sem.at[index])
        for index, (source, target) in enumerate(
            (
                (wuk_hbm, wuk),
                (slat_hbm, slat),
                (srope_hbm, srope),
                (wuv_hbm, wuv),
                (plat_hbm.at[0], plat),
                (prope_hbm.at[0], prope),
                (wout_hbm, wout),
            )
        )
    ]
    for load in loads:
        load.start()
    load_wuk, load_slat, load_srope, load_wuv, load_plat, load_prope, load_wout = loads

    for s in range(samples):
        tok[2 * s : 2 * s + 2, :] = q_ref[s].astype(F32)
    for h in range(heads):
        qf[pl.ds(h, pairs, stride=wide), :] = tok[:, h * NOPE : (h + 1) * NOPE]
    for s in range(samples):
        tok[2 * s : 2 * s + 2, : heads * ROPE] = r_ref[s].astype(F32)
    low = iota((pairs, NOPE), 1) < ROPE
    for h in range(heads):
        both = tok[:, h // 2 * NOPE : (h // 2 + 1) * NOPE]
        if h % 2 == 1:
            both = pltpu.roll(both, ROPE, 1)
        qf[pl.ds(heads + h, pairs, stride=wide), :] = jnp.where(low, both, 1.0)
    for s in range(samples):
        qb[s] = qf[2 * wide * s : 2 * wide * (s + 1), :].astype(BF16)
    qb[samples] = jnp.zeros(qb.shape[1:], BF16)

    pl.semaphore_wait(barrier, slots - 1 + nh - 1)

    def query_copy(k):
        to_z, to_y = ahead(k)
        return pltpu.make_async_remote_copy(
            src_ref=sb.at[k],
            dst_ref=rb.at[k],
            send_sem=q_send.at[k],
            recv_sem=q_recv.at[k],
            device_id={"prompt": to_z, "sample": to_y},
            device_id_type=MESH,
        )

    names = [sp_ref[s] for s in range(samples)]

    def sample_for(owner):
        found = samples
        for s in range(samples):
            found = jnp.where(names[s] == owner, s, found)
        return found

    for k in range(1, slots):
        to_z, to_y = ahead(k)
        sb[k] = qb[sample_for(to_z * ny + to_y)]
        query_copy(k).start()
    rb[0] = qb[sample_for(here)]

    side = 8 * pairs
    for s in range(samples):
        ntok[2 * s : 2 * s + 2, :LAT] = nl_ref[s].astype(F32)
        ntok[2 * s : 2 * s + 2, LAT:] = jnp.zeros((2, NOPE), F32)
        ntok[2 * s : 2 * s + 2, LAT : LAT + ROPE] = nr_ref[s].astype(F32)
    for g in range(2):
        for h in range(half, 8):
            lrf[pl.ds(g * side + h, pairs, stride=8), :] = jnp.zeros((pairs, NOPE), F32)
            put(lqf, g * side + h, pairs, 8, jnp.zeros((pairs, LAT), F32))
    load_wuk.wait()
    for g in range(2):
        for h in range(half):
            rows = qf[pl.ds(g * half + h, pairs, stride=wide), :].astype(BF16)
            put(lqf, g * side + h, pairs, 8, dot(rows, wuk[g * half + h]))
            rope_rows = qf[pl.ds(heads + g * half + h, pairs, stride=wide), :]
            lrf[pl.ds(g * side + h, pairs, stride=8), :] = jnp.where(low, rope_rows, 0.0)
    load_slat.wait()
    load_srope.wait()
    lane = iota((32, 128), 1)
    spans = [(slice(16 * s, 16 * s + 16), slice(side + 16 * s, side + 16 * s + 16)) for s in range(samples)]
    for s, (top, bottom) in enumerate(spans):
        lat_rows = jnp.concatenate([whole(lqf, top), whole(lqf, bottom)], axis=0).astype(BF16)
        rope_rows = jnp.concatenate([lrf[top, :], lrf[bottom, :]], axis=0).astype(BF16)[:, :ROPE]
        scores = dot_nt(lat_rows, slat[s]) + dot(rope_rows, srope[s])
        scores = jnp.where(lane < len_ref[s], scores, FLOOR)
        lsc[top, :] = scores[:16]
        lsc[bottom, :] = scores[16:]
    new_latent = ntok[:, :LAT].astype(BF16)
    new_rope = ntok[:, LAT:].astype(BF16)
    count = 2 * side
    new_scores = dot_nt(whole(lqf).astype(BF16), new_latent) + dot_nt(
        lrf[...].astype(BF16), new_rope
    )
    row, key = iota((count, pairs), 0), iota((count, pairs), 1)
    row = jnp.where(row >= side, row - side, row)
    valid = ((key >> 1) == (row >> 4)) & ((key & 1) <= ((row >> 3) & 1))
    new_scores = jnp.where(valid, new_scores, FLOOR)
    old_scores = lsc[...]
    peak = jnp.maximum(
        jnp.max(old_scores, axis=1, keepdims=True), jnp.max(new_scores, axis=1, keepdims=True)
    )
    old_exp = jnp.exp2((old_scores - peak) * EXP2_SCALE)
    new_exp = jnp.exp2((new_scores - peak) * EXP2_SCALE)
    total = jnp.sum(old_exp, axis=1, keepdims=True) + jnp.sum(new_exp, axis=1, keepdims=True)
    lse_col[...] = jnp.broadcast_to(peak * SCALE + jnp.log(total), lse_col.shape)
    lsc[...] = old_exp
    new_out = dot(new_exp.astype(BF16), new_latent)
    inverse = 1.0 / total
    for s, (top, bottom) in enumerate(spans):
        probs = jnp.concatenate([lsc[top, :], lsc[bottom, :]], axis=0).astype(BF16)
        own_out = dot(probs, slat[s])
        fill(lof, (new_out[top] + own_out[:16]) * inverse[top], top)
        fill(lof, (new_out[bottom] + own_out[16:]) * inverse[bottom], bottom)
    load_wuv.wait()
    for g in range(2):
        for h in range(half):
            rows = take(lof, g * side + h, pairs, 8).astype(BF16)
            lvf[pl.ds(g * side + h, pairs, stride=8), :] = dot(rows, wuv[g * half + h])
        for h in range(half, 8):
            lvf[pl.ds(g * side + h, pairs, stride=8), :] = jnp.zeros((pairs, VDIM), F32)
            rvf[g, pl.ds(h, spots, stride=8), :] = jnp.zeros((spots, VDIM), F32)

    def back_copy(g, k):
        to_z, to_y = behind(k)
        return pltpu.make_async_remote_copy(
            src_ref=back.at[g, k],
            dst_ref=(rr0, rr1)[g].at[here],
            send_sem=b_send.at[g, k],
            recv_sem=b_recv.at[g, k],
            device_id={"prompt": to_z, "sample": to_y},
            device_id_type=MESH,
        )

    load_plat.wait()
    load_prope.wait()
    for k in range(1, slots):
        query_copy(k).wait_recv()
    xf[...] = rb[...].astype(F32).reshape(xf.shape)
    flags = pltpu.roll(xf[pl.ds(heads, spots, stride=wide), :], ROPE, 1)
    down, across = iota((spots, spots), 0), iota((spots, spots), 1)
    before = jnp.where(((across & 1) == 0) & ((across >> 1) < (down >> 1)), 1.0, 0.0)
    rank_down = dot(before.astype(BF16), flags.astype(BF16))[:, :used]
    down, across = iota((spots, used), 0), iota((spots, used), 1)
    unpick = jnp.where(
        (flags[:, :used] > 0.5)
        & (rank_down == (across >> 1).astype(F32))
        & ((across & 1) == (down & 1)),
        1.0,
        0.0,
    ).astype(BF16)
    down, across = iota((spots, spots), 0), iota((spots, spots), 1)
    after = ((down & 1) == 0) & ((down >> 1) < (across >> 1))
    square = flags[:, :spots]
    ones = jnp.ones((used, spots), BF16)
    rank_across = dot(ones, jnp.where(after, square, 0.0).astype(BF16))
    flag_across = dot(ones, jnp.where(down == across, square, 0.0).astype(BF16))
    down, across = iota((used, spots), 0), iota((used, spots), 1)
    pick = jnp.where(
        (flag_across > 0.5)
        & (rank_across == (down >> 1).astype(F32))
        & ((across & 1) == (down & 1)),
        1.0,
        0.0,
    ).astype(BF16)
    rows_all = used * half
    down, across = iota((used, rows_all), 0) * half, iota((used, rows_all), 1)
    gather_rows = jnp.where((across >= down) & (across < down + half), 1.0, 0.0).astype(BF16)
    stat_pick = dot(unpick, gather_rows).astype(BF16)
    length = plat.shape[0]
    tile = min(512, length)
    for g in range(2):
        for h in range(half):
            at = g * half + h
            both = jnp.concatenate(
                [
                    xf[pl.ds(at, spots, stride=wide), :],
                    xf[pl.ds(heads + at, spots, stride=wide), :],
                ],
                axis=1,
            ).astype(BF16)
            both = dot(pick, both)
            put(plf.at[g], h, used, half, dot(both[:, :NOPE].astype(BF16), wuk[at]))
            prf[g, pl.ds(h, used, stride=half), :] = both[:, NOPE:]
        lat_rows = whole(plf.at[g]).astype(BF16)
        rope_rows = prf[g].astype(BF16)[:, :ROPE]
        top = None
        for at in range(0, length, tile):
            scores = dot_nt(lat_rows, plat[at : at + tile, :]) + dot(
                rope_rows, prope[:, at : at + tile]
            )
            sc[g, :, at : at + tile] = scores
            for lanes in range(0, tile, 128):
                piece = scores[:, lanes : lanes + 128]
                top = piece if top is None else jnp.maximum(top, piece)
        peak = jnp.max(top, axis=1, keepdims=True)
        sums_of = jnp.zeros((rows_all, 128), F32)
        for at in range(0, length, tile):
            probs = jnp.exp2((sc[g, :, at : at + tile] - peak) * EXP2_SCALE)
            for lanes in range(0, tile, 128):
                sums_of = sums_of + probs[:, lanes : lanes + 128]
            pb[g, :, at : at + tile] = probs.astype(BF16)
        total = jnp.sum(sums_of, axis=1, keepdims=True)
        fill(pof.at[g], dot(pb[g], plat[...]) * (1.0 / total))
        for h in range(half):
            rows = take(pof.at[g], h, used, half).astype(BF16)
            head_values = dot(rows, wuv[g * half + h]).astype(BF16)
            rvf[g, pl.ds(h, spots, stride=8), :] = dot(unpick, head_values)
        lse = peak * SCALE + jnp.log(total)
        first = lse.astype(BF16).astype(F32)
        second = (lse - first).astype(BF16).astype(F32)
        third = lse - first - second
        row, lane = iota((rows_all, 128), 0), iota((rows_all, 128), 1)
        place = row - half * ((row * 43691) >> 18)
        spread = (
            jnp.where(lane == place, first, 0.0)
            + jnp.where(lane == place + 16, second, 0.0)
            + jnp.where(lane == place + 32, third, 0.0)
        ).astype(BF16)
        rvf[g, pl.ds(half, spots, stride=8), :] = dot(stat_pick, spread)
        back[g] = rvf[g].reshape(slots, 16, VDIM).astype(BF16)
        for k in range(1, slots):
            back_copy(g, k).start()
        (rr0, rr1)[g][here] = back[g, 0]

    def value_copy(g, d):
        return pltpu.make_async_remote_copy(
            src_ref=vg.at[g, y],
            dst_ref=vg.at[g, y],
            send_sem=v_send.at[g, d],
            recv_sem=v_recv.at[g, d],
            device_id={"sample": y_at[d]},
            device_id_type=MESH,
        )

    third_of = half // 2
    row, lane = iota((8, 128), 0), iota((8, 128), 1)
    mine = (lane == row) | (lane == row + 16) | (lane == row + 32)
    for g in range(2):
        for k in range(1, slots):
            back_copy(g, k).wait_recv()
        for s in range(samples):
            cf[16 * s : 16 * s + 16, :] = (rr0, rr1)[g][names[s]].astype(F32)
        for pair in range(pairs):
            rows = slice(8 * pair, 8 * pair + 8)
            local_rows = slice(g * side + 8 * pair, g * side + 8 * pair + 8)
            stat = jnp.broadcast_to(cf[8 * pair + half : 8 * pair + half + 1, :], (8, 128))
            lse_prompt = jnp.sum(jnp.where(mine, stat, 0.0), axis=1, keepdims=True)
            lse_local = lse_col[local_rows, :]
            top = jnp.maximum(lse_prompt, lse_local)
            weight_prompt = jnp.exp(lse_prompt - top)
            weight_local = jnp.exp(lse_local - top)
            lvf[local_rows, :] = (
                weight_prompt * cf[rows, :] + weight_local * lvf[local_rows, :]
            ) / (weight_prompt + weight_local)
        columns = [
            jnp.concatenate(
                [
                    lvf[pl.ds(g * side + h, pairs, stride=8), :],
                    lvf[pl.ds(g * side + h + third_of, pairs, stride=8), :],
                ],
                axis=0,
            )
            for h in range(third_of)
        ]
        vg[g, y] = jnp.concatenate(columns, axis=1).astype(BF16)
        for d in range(1, ny):
            value_copy(g, d).start()

    def sum_copy(j):
        return pltpu.make_async_remote_copy(
            src_ref=blocks.at[j],
            dst_ref=sums.at[head],
            send_sem=o_send.at[j],
            recv_sem=o_recv.at[head],
            device_id={"head": j},
            device_id_type=MESH,
        )

    for k in range(1, slots):
        query_copy(k).wait_send()
    load_wout.wait()
    columns_all = wout.shape[1]
    width = columns_all // nh
    inner = half * VDIM
    done = 0
    tile = 256
    for g in range(2):
        for d in range(1, ny):
            value_copy(g, d).wait_recv()
        for d in range(ny):
            gathered = vg[g, d].astype(F32)
            lhs[pairs * d : pairs * (d + 1), : inner // 2] = gathered[:pairs]
            lhs[pairs * d : pairs * (d + 1), inner // 2 :] = gathered[pairs:]
        left = lhs[...].astype(BF16)
        for at in range(0, columns_all, tile):
            stop = min(at + tile, columns_all)
            product = dot(left, wout[g * inner : (g + 1) * inner, at:stop])
            if g == 0:
                part[:, at:stop] = product
                continue
            part[:, at:stop] = part[:, at:stop] + product
            while done < nh and (done + 1) * width <= stop:
                start = done * width
                floor = start // 128 * 128
                ceil = min(-(-(start + width) // 128) * 128, columns_all)
                block = part[:, floor:ceil]
                if start > floor:
                    block = pltpu.roll(block, ceil - start, 1)
                blocks[done] = block[:, :width].astype(BF16)

                @pl.when(head != done)
                def _(j=done):
                    sum_copy(j).start()

                done += 1

    for g in range(2):
        for k in range(1, slots):
            back_copy(g, k).wait_send()
        for d in range(1, ny):
            value_copy(g, d).wait_send()
    result = blocks[head].astype(F32)
    for d in range(1, nh):
        source = head_at[d]
        pltpu.make_async_remote_copy(
            src_ref=blocks.at[source],
            dst_ref=sums.at[source],
            send_sem=o_send.at[source],
            recv_sem=o_recv.at[source],
            device_id={"head": source},
            device_id_type=MESH,
        ).wait_recv()
        result = result + sums[source].astype(F32)
    final[...] = result
    for row in range(ny * samples):
        out_ref[row] = final[2 * row : 2 * row + 2, :].astype(BF16)
    for d in range(1, nh):
        sum_copy(head_at[d]).wait_send()


def shards(
    q_nope,
    q_rope,
    new_latent,
    new_rope,
    prompt_latent,
    prompt_rope,
    suffix_latent,
    suffix_rope,
    sample_prompt,
    suffix_len,
    w_uk,
    w_uv,
    w_out,
):
    nz, ny, nh = (lax.axis_size(name) for name in ("prompt", "sample", "head"))
    slots = nz * ny
    samples = q_nope.shape[0]
    pairs = 2 * samples
    heads = w_uk.shape[0]
    length = prompt_latent.shape[1]
    width = w_out.shape[1] // nh
    half = heads // 2
    used = 2 * min(MOST, slots)
    rows_all = used * half
    count = 16 * pairs
    vmem = pltpu.VMEM
    dma = pltpu.SemaphoreType.DMA
    in_vmem = pl.BlockSpec(memory_space=pltpu.VMEM)
    in_smem = pl.BlockSpec(memory_space=pltpu.SMEM)
    in_hbm = pl.BlockSpec(memory_space=pl.ANY)
    return pl.pallas_call(
        functools.partial(kernel, (nz, ny, nh)),
        out_shape=jax.ShapeDtypeStruct((samples * ny, 2, width), BF16),
        in_specs=[in_smem] * 2 + [in_vmem] * 4 + [in_hbm] * 7,
        out_specs=in_vmem,
        scratch_shapes=[
            vmem(prompt_latent.shape[1:], BF16),
            vmem(prompt_rope.shape[1:], BF16),
            vmem(suffix_latent.shape, BF16),
            vmem(suffix_rope.shape, BF16),
            vmem(w_uk.shape, BF16),
            vmem(w_uv.shape, BF16),
            vmem(w_out.shape, BF16),
            vmem((pairs, heads * NOPE), F32),
            vmem((pairs, LAT + NOPE), F32),
            vmem((pairs * 2 * heads, NOPE), F32),
            vmem((samples + 1, 4 * heads, NOPE), BF16),
            vmem((slots, 4 * heads, NOPE), BF16),
            vmem((slots, 4 * heads, NOPE), BF16),
            vmem((slots * 4 * heads, NOPE), F32),
            vmem((LAT // 128, count, 128), F32),
            vmem((count, NOPE), F32),
            vmem((count, suffix_latent.shape[1]), F32),
            vmem((LAT // 128, count, 128), F32),
            vmem((count, VDIM), F32),
            vmem((count, VDIM), F32),
            vmem((2, LAT // 128, rows_all, 128), F32),
            vmem((2, rows_all, NOPE), F32),
            vmem((2, rows_all, length), F32),
            vmem((2, rows_all, length), BF16),
            vmem((2, LAT // 128, rows_all, 128), F32),
            vmem((2, 16 * slots, VDIM), F32),
            vmem((2, slots, 16, VDIM), BF16),
            vmem((slots, 16, VDIM), BF16),
            vmem((slots, 16, VDIM), BF16),
            vmem((8 * pairs, VDIM), F32),
            vmem((2, ny, 2 * pairs, half * VDIM // 2), BF16),
            vmem((ny * pairs, half * VDIM), F32),
            vmem((ny * pairs, w_out.shape[1]), F32),
            vmem((nh, ny * pairs, width), BF16),
            vmem((nh, ny * pairs, width), BF16),
            vmem((ny * pairs, width), F32),
            dma((7,)),
            dma((slots,)),
            dma((slots,)),
            dma((2, slots)),
            dma((2, slots)),
            dma((2, ny)),
            dma((2, ny)),
            dma((nh,)),
            dma((nh,)),
        ],
        compiler_params=pltpu.CompilerParams(
            collective_id=0, has_side_effects=True, vmem_limit_bytes=56 * 1024 * 1024
        ),
        cost_estimate=pl.CostEstimate(
            flops=5 * 10**9, bytes_accessed=13 * 10**6, transcendentals=2 * 10**6
        ),
    )(
        sample_prompt,
        suffix_len,
        q_nope,
        q_rope,
        new_latent,
        new_rope,
        prompt_latent,
        prompt_rope,
        suffix_latent,
        suffix_rope,
        w_uk,
        w_uv,
        w_out,
    )


def solution(mesh):
    placed = (
        P(("prompt", "sample"), None, "head"),
        P(("prompt", "sample"), None, "head"),
        P(("prompt", "sample"), None, None),
        P(("prompt", "sample"), None, None),
        P(("prompt", "sample"), None, None),
        P(("prompt", "sample"), None, None),
        P(("prompt", "sample"), None, None),
        P(("prompt", "sample"), None, None),
        P(("prompt", "sample")),
        P(("prompt", "sample")),
        P("head", None, None),
        P("head", None, None),
        P("head", "sample"),
    )
    return jax.shard_map(
        shards,
        mesh=mesh,
        in_specs=placed,
        out_specs=P("prompt", None, ("sample", "head")),
        check_vma=False,
    )
```

time: 52 us -> 53.1 us (1.021)
  Pallas kernels: 49.8 us -> 51.4 us
    pallas_call x1, Pallas kernels: 49.8 us -> 51.4 us  [shards(): pl.pallas_call(functools.partial(kernel, (nz, ny, nh)), out_shape=jax.Sha...]
    unnamed x0 -> x1, local copies, waits for them, and re-layouts: none -> 1.45 us
    reshape x1 -> x0, local copies, waits for them, and re-layouts: 1.45 us -> none  [shards(): return result.reshape(ny * samples, 2, width)]
where the time goes in v2:
time: 53.1 us; the launch traced here: 52.9 us
  Pallas kernels  51.4 us (97%)
  local copies, waits for them, and re-layouts  1.45 us (3%)
    pallas_call x1, Pallas kernels, shards(): pl.pallas_call(functools.partial(kernel, (nz, ny, nh)), out_shape=jax.Sha...  51.4 us
    unnamed x1, local copies, waits for them, and re-layouts  1.45 us

profile of v2, /device:TPU:1, one launch (start us, length us, event | category | flops | bytes accessed | tf_op | source)
XLA Modules:
  0.0 52.9 jit_solution(7918674946654604675)
XLA Ops:
  0.0 51.4 %shard_map.127 = bf16[48,2,224]{2,1,0:T(2,128)(2,1)} custom-call(s32[12]{0:T(128)} %sp_ref.1, s32[12]{0:T(128)} %len_ref.1, bf16[12,2,1536]{2,1,0:T(2,128)(2,1)} %q_ref.1, bf16[12,2,768]{2,1,0:T(2,128)(2,1)} %r_ref.1, bf16[12,2,512]{2,1,0:T(2,128)(2,1)} %nl_ref.1, bf16[12,2,64]{2,1,0:T(2,128)(2,1)} %nr_ref.1, bf16[1,2048,512]{2,1,0:T(8,128)(2,1)} %plat_hbm.1, ...), custom_call_target="tpu_custom_call" | custom-call | flops 5000000000 | bytes 13000000 | tf_op jit(solution)/shard_map/pallas_call | solution.py:528
  51.5 1.5 %copy.15 = bf16[48,2,224]{2,1,0:T(2,128)(2,1)} copy(bf16[48,2,224]{2,1,0:T(2,128)(2,1)} %shard_map.127) | data formatting | bytes 86016

commit v3 on v1

v3 whole, which is shorter than its diff:
```python
import functools
import math

import jax
import jax.numpy as jnp
from jax import lax
from jax.experimental import pallas as pl
from jax.experimental.pallas import tpu as pltpu
from jax.sharding import PartitionSpec as P

NOPE = 128
ROPE = 64
LAT = 512
VDIM = 128
F32 = jnp.float32
BF16 = jnp.bfloat16
MESH = pl.DeviceIdType.MESH
FLOOR = -1e30
SCALE = 1.0 / math.sqrt(NOPE + ROPE)
EXP2_SCALE = SCALE * math.log2(math.e)
MOST = 16
NT = (((1,), (1,)), ((), ()))


def dot(left, right):
    return jnp.dot(left, right, preferred_element_type=F32)


def dot_nt(left, right):
    return lax.dot_general(left, right, NT, preferred_element_type=F32)


def put(ref, first, count, stride, value):
    for tile in range(ref.shape[0]):
        ref[tile, pl.ds(first, count, stride=stride), :] = value[:, 128 * tile : 128 * (tile + 1)]


def take(ref, first, count, stride):
    tiles = [ref[tile, pl.ds(first, count, stride=stride), :] for tile in range(ref.shape[0])]
    return jnp.concatenate(tiles, axis=1)


def whole(ref, rows=slice(None)):
    return jnp.concatenate([ref[tile, rows, :] for tile in range(ref.shape[0])], axis=1)


def fill(ref, value, rows=slice(None)):
    for tile in range(ref.shape[0]):
        ref[tile, rows, :] = value[:, 128 * tile : 128 * (tile + 1)]


def iota(shape, axis):
    return lax.broadcasted_iota(jnp.int32, shape, axis)


def kernel(
    sizes,
    sp_ref,
    len_ref,
    q_hbm,
    r_hbm,
    nl_hbm,
    nr_hbm,
    plat_hbm,
    prope_hbm,
    slat_hbm,
    srope_hbm,
    wuk_hbm,
    wuv_hbm,
    wout_hbm,
    out_ref,
    q_ref,
    r_ref,
    nl_ref,
    nr_ref,
    plat,
    prope,
    slat,
    srope,
    wuk,
    wuv,
    wout,
    tok,
    ntok,
    qf,
    qb,
    sb,
    rb,
    xf,
    lqf,
    lrf,
    lsc,
    lnew,
    linv,
    lof,
    lvf,
    lse_col,
    plf,
    prf,
    sc,
    pb,
    pof,
    rvf,
    back,
    rr,
    cf,
    vg,
    lhs,
    part,
    keep,
    blocks,
    pair_in,
    chip_sum,
    sums,
    final,
    load_sem,
    ready,
    q_send,
    q_recv,
    b_send,
    b_recv,
    v_send,
    v_recv,
    p_send,
    p_recv,
    o_send,
    o_recv,
):
    nz, ny, nh = sizes
    nx = nh // 2
    slots = nz * ny
    samples = q_ref.shape[0]
    pairs = 2 * samples
    heads = wuk.shape[0]
    wide = 2 * heads
    spots = 2 * slots
    used = 2 * min(MOST, slots)
    z = lax.axis_index("prompt")
    y = lax.axis_index("sample")
    head = lax.axis_index("head")
    core = lax.rem(head, 2)
    x = head // 2
    here = z * ny + y
    z_at = [lax.rem(z + d, nz) for d in range(nz)]
    y_at = [lax.rem(y + d, ny) for d in range(ny)]
    x_at = [lax.rem(x + d, nx) for d in range(nx)]
    mate = head + 1 - 2 * core

    def ahead(k):
        step = k // ny
        away = (step + 1) // 2
        return z_at[away if step % 2 == 1 else (nz - away) % nz], y_at[k % ny]

    def behind(k):
        step = k // ny
        away = (step + 1) // 2
        return z_at[(nz - away) % nz if step % 2 == 1 else away], y_at[(ny - k % ny) % ny]

    barrier = pltpu.get_barrier_semaphore()
    near = (
        [{"prompt": z_at[d]} for d in range(1, nz)]
        + [{"sample": y_at[d]} for d in range(1, ny)]
        + [{"head": mate}]
        + [{"head": 2 * x_at[d] + core} for d in range(1, nx)]
    )
    for device in near:
        pl.semaphore_signal(barrier, inc=1, device_id=device, device_id_type=MESH)

    loads = [
        pltpu.make_async_copy(source, target, load_sem.at[index])
        for index, (source, target) in enumerate(
            (
                (q_hbm, q_ref),
                (r_hbm, r_ref),
                (nl_hbm, nl_ref),
                (nr_hbm, nr_ref),
                (wuk_hbm, wuk),
                (slat_hbm, slat),
                (srope_hbm, srope),
                (plat_hbm.at[0], plat),
                (prope_hbm.at[0], prope),
                (wuv_hbm, wuv),
                (wout_hbm, wout),
            )
        )
    ]
    for load in loads:
        load.start()

    loads[0].wait()
    for s in range(samples):
        tok[2 * s : 2 * s + 2, :] = q_ref[s].astype(F32)
    for h in range(heads):
        qf[pl.ds(h, pairs, stride=wide), :] = tok[:, h * NOPE : (h + 1) * NOPE]
    loads[1].wait()
    for s in range(samples):
        tok[2 * s : 2 * s + 2, : heads * ROPE] = r_ref[s].astype(F32)
    low = iota((pairs, NOPE), 1) < ROPE
    for h in range(heads):
        both = tok[:, h // 2 * NOPE : (h // 2 + 1) * NOPE]
        if h % 2 == 1:
            both = pltpu.roll(both, ROPE, 1)
        qf[pl.ds(heads + h, pairs, stride=wide), :] = jnp.where(low, both, 1.0)
    for s in range(samples):
        qb[s] = qf[2 * wide * s : 2 * wide * (s + 1), :].astype(BF16)
    qb[samples] = jnp.zeros(qb.shape[1:], BF16)

    pl.semaphore_wait(barrier, len(near))
    for d in range(1, ny):
        pl.semaphore_signal(ready, inc=1, device_id={"sample": y_at[d]}, device_id_type=MESH)
    pl.semaphore_wait(ready, ny - 1)

    def query_copy(k):
        to_z, to_y = ahead(k)
        return pltpu.make_async_remote_copy(
            src_ref=sb.at[k],
            dst_ref=rb.at[k],
            send_sem=q_send.at[k],
            recv_sem=q_recv.at[k],
            device_id={"prompt": to_z, "sample": to_y},
            device_id_type=MESH,
        )

    names = [sp_ref[s] for s in range(samples)]

    def sample_for(owner):
        found = samples
        for s in range(samples):
            found = jnp.where(names[s] == owner, s, found)
        return found

    for k in range(1, slots):
        to_z, to_y = ahead(k)
        sb[k] = qb[sample_for(to_z * ny + to_y)]
        query_copy(k).start()
    rb[0] = qb[sample_for(here)]

    loads[2].wait()
    loads[3].wait()
    for s in range(samples):
        ntok[2 * s : 2 * s + 2, :LAT] = nl_ref[s].astype(F32)
        ntok[2 * s : 2 * s + 2, LAT:] = jnp.zeros((2, NOPE), F32)
        ntok[2 * s : 2 * s + 2, LAT : LAT + ROPE] = nr_ref[s].astype(F32)
    for h in range(heads, 16):
        lrf[pl.ds(h, pairs, stride=16), :] = jnp.zeros((pairs, NOPE), F32)
        put(lqf, h, pairs, 16, jnp.zeros((pairs, LAT), F32))
    loads[4].wait()
    for h in range(heads):
        rows = qf[pl.ds(h, pairs, stride=wide), :].astype(BF16)
        put(lqf, h, pairs, 16, dot(rows, wuk[h]))
        rope_rows = qf[pl.ds(heads + h, pairs, stride=wide), :]
        lrf[pl.ds(h, pairs, stride=16), :] = jnp.where(low, rope_rows, 0.0)
    loads[5].wait()
    loads[6].wait()
    lane = iota((32, 128), 1)
    for s in range(samples):
        rows = slice(32 * s, 32 * s + 32)
        scores = dot_nt(whole(lqf, rows).astype(BF16), slat[s]) + dot(
            lrf[rows, :].astype(BF16)[:, :ROPE], srope[s]
        )
        lsc[rows, :] = jnp.where(lane < len_ref[s], scores, FLOOR)
    new_latent = ntok[:, :LAT].astype(BF16)
    new_rope = ntok[:, LAT:].astype(BF16)
    count = 16 * pairs
    new_scores = dot_nt(whole(lqf).astype(BF16), new_latent) + dot_nt(
        lrf[...].astype(BF16), new_rope
    )
    row, key = iota((count, pairs), 0), iota((count, pairs), 1)
    valid = ((key >> 1) == (row >> 5)) & ((key & 1) <= ((row >> 4) & 1))
    new_scores = jnp.where(valid, new_scores, FLOOR)
    old_scores = lsc[...]
    peak = jnp.maximum(
        jnp.max(old_scores, axis=1, keepdims=True), jnp.max(new_scores, axis=1, keepdims=True)
    )
    old_exp = jnp.exp2((old_scores - peak) * EXP2_SCALE)
    new_exp = jnp.exp2((new_scores - peak) * EXP2_SCALE)
    total = jnp.sum(old_exp, axis=1, keepdims=True) + jnp.sum(new_exp, axis=1, keepdims=True)
    lse_col[...] = jnp.broadcast_to(peak * SCALE + jnp.log(total), lse_col.shape)
    linv[...] = jnp.broadcast_to(1.0 / total, linv.shape)
    lsc[...] = old_exp
    lnew[...] = new_exp

    def back_copy(k):
        to_z, to_y = behind(k)
        return pltpu.make_async_remote_copy(
            src_ref=back.at[k],
            dst_ref=rr.at[here],
            send_sem=b_send.at[k],
            recv_sem=b_recv.at[k],
            device_id={"prompt": to_z, "sample": to_y},
            device_id_type=MESH,
        )

    for h in range(heads, 16):
        rvf[pl.ds(h, spots, stride=16), :] = jnp.zeros((spots, VDIM), F32)
    for load in loads[7:10]:
        load.wait()
    for k in range(1, slots):
        query_copy(k).wait_recv()
    xf[...] = rb[...].astype(F32).reshape(xf.shape)
    flags = pltpu.roll(xf[pl.ds(heads, spots, stride=wide), :], ROPE, 1)
    down, across = iota((spots, spots), 0), iota((spots, spots), 1)
    before = jnp.where(((across & 1) == 0) & ((across >> 1) < (down >> 1)), 1.0, 0.0)
    rank_down = dot(before.astype(BF16), flags.astype(BF16))[:, :used]
    down, across = iota((spots, used), 0), iota((spots, used), 1)
    unpick = jnp.where(
        (flags[:, :used] > 0.5)
        & (rank_down == (across >> 1).astype(F32))
        & ((across & 1) == (down & 1)),
        1.0,
        0.0,
    ).astype(BF16)
    down, across = iota((spots, spots), 0), iota((spots, spots), 1)
    after = ((down & 1) == 0) & ((down >> 1) < (across >> 1))
    square = flags[:, :spots]
    ones = jnp.ones((used, spots), BF16)
    rank_across = dot(ones, jnp.where(after, square, 0.0).astype(BF16))
    flag_across = dot(ones, jnp.where(down == across, square, 0.0).astype(BF16))
    down, across = iota((used, spots), 0), iota((used, spots), 1)
    pick = jnp.where(
        (flag_across > 0.5)
        & (rank_across == (down >> 1).astype(F32))
        & ((across & 1) == (down & 1)),
        1.0,
        0.0,
    ).astype(BF16)
    rows_all = used * heads
    down, across = iota((used, rows_all), 0) * heads, iota((used, rows_all), 1)
    gather_rows = jnp.where((across >= down) & (across < down + heads), 1.0, 0.0).astype(BF16)
    stat_pick = dot(unpick, gather_rows).astype(BF16)
    length = plat.shape[0]
    tile = min(512, length)
    for h in range(heads):
        both = jnp.concatenate(
            [xf[pl.ds(h, spots, stride=wide), :], xf[pl.ds(heads + h, spots, stride=wide), :]],
            axis=1,
        ).astype(BF16)
        both = dot(pick, both)
        put(plf, h, used, heads, dot(both[:, :NOPE].astype(BF16), wuk[h]))
        prf[pl.ds(h, used, stride=heads), :] = both[:, NOPE:]
    lat_rows = whole(plf).astype(BF16)
    rope_rows = prf[...].astype(BF16)[:, :ROPE]
    top = None
    for at in range(0, length, tile):
        scores = dot_nt(lat_rows, plat[at : at + tile, :]) + dot(
            rope_rows, prope[:, at : at + tile]
        )
        sc[:, at : at + tile] = scores
        for lanes in range(0, tile, 128):
            piece = scores[:, lanes : lanes + 128]
            top = piece if top is None else jnp.maximum(top, piece)
    peak = jnp.max(top, axis=1, keepdims=True)
    sums_of = jnp.zeros((rows_all, 128), F32)
    for at in range(0, length, tile):
        probs = jnp.exp2((sc[:, at : at + tile] - peak) * EXP2_SCALE)
        for lanes in range(0, tile, 128):
            sums_of = sums_of + probs[:, lanes : lanes + 128]
        pb[:, at : at + tile] = probs.astype(BF16)
    total = jnp.sum(sums_of, axis=1, keepdims=True)
    fill(pof, dot(pb[...], plat[...]) * (1.0 / total))
    for h in range(heads):
        head_values = dot(take(pof, h, used, heads).astype(BF16), wuv[h]).astype(BF16)
        rvf[pl.ds(h, spots, stride=16), :] = dot(unpick, head_values)
    lse = peak * SCALE + jnp.log(total)
    first = lse.astype(BF16).astype(F32)
    second = (lse - first).astype(BF16).astype(F32)
    third = lse - first - second
    row, lane = iota((rows_all, 128), 0), iota((rows_all, 128), 1)
    place = row - heads * ((row * 43691) >> 19)
    spread = (
        jnp.where(lane == place, first, 0.0)
        + jnp.where(lane == place + 16, second, 0.0)
        + jnp.where(lane == place + 32, third, 0.0)
    ).astype(BF16)
    rvf[pl.ds(heads, spots, stride=16), :] = dot(stat_pick, spread)
    back[...] = rvf[...].reshape(slots, 32, VDIM).astype(BF16)
    for k in range(1, slots):
        back_copy(k).start()
    rr[here] = back[0]

    new_out = dot(lnew[...].astype(BF16), ntok[:, :LAT].astype(BF16))
    for s in range(samples):
        rows = slice(32 * s, 32 * s + 32)
        own_out = new_out[rows] + dot(lsc[rows, :].astype(BF16), slat[s])
        fill(lof, own_out * linv[rows, :1], rows)
    for h in range(heads):
        lvf[pl.ds(h, pairs, stride=16), :] = dot(take(lof, h, pairs, 16).astype(BF16), wuv[h])
    for h in range(heads, 16):
        lvf[pl.ds(h, pairs, stride=16), :] = jnp.zeros((pairs, VDIM), F32)
    for k in range(1, slots):
        query_copy(k).wait_send()
    loads[10].wait()
    for k in range(1, slots):
        back_copy(k).wait_recv()

    for s in range(samples):
        cf[32 * s : 32 * s + 32, :] = rr[names[s]].astype(F32)
    row, lane = iota((16, 128), 0), iota((16, 128), 1)
    mine = (lane == row) | (lane == row + 16) | (lane == row + 32)
    for pair in range(pairs):
        rows = slice(16 * pair, 16 * pair + 16)
        stat = jnp.broadcast_to(cf[16 * pair + heads : 16 * pair + heads + 1, :], (16, 128))
        lse_prompt = jnp.sum(jnp.where(mine, stat, 0.0), axis=1, keepdims=True)
        lse_local = lse_col[rows, :]
        top = jnp.maximum(lse_prompt, lse_local)
        weight_prompt = jnp.exp(lse_prompt - top)
        weight_local = jnp.exp(lse_local - top)
        lvf[rows, :] = (weight_prompt * cf[rows, :] + weight_local * lvf[rows, :]) / (
            weight_prompt + weight_local
        )
    half = heads // 2
    columns = [
        jnp.concatenate(
            [lvf[pl.ds(h, pairs, stride=16), :], lvf[pl.ds(h + half, pairs, stride=16), :]], axis=0
        )
        for h in range(half)
    ]
    vg[y] = jnp.concatenate(columns, axis=1).astype(BF16)

    def value_copy(d):
        return pltpu.make_async_remote_copy(
            src_ref=vg.at[y],
            dst_ref=vg.at[y],
            send_sem=v_send.at[d],
            recv_sem=v_recv.at[d],
            device_id={"sample": y_at[d]},
            device_id_type=MESH,
        )

    for d in range(1, ny):
        value_copy(d).start()
    for k in range(1, slots):
        back_copy(k).wait_send()
    for d in range(1, ny):
        value_copy(d).wait_recv()

    for d in range(ny):
        gathered = vg[d].astype(F32)
        lhs[pairs * d : pairs * (d + 1), : half * VDIM] = gathered[:pairs]
        lhs[pairs * d : pairs * (d + 1), half * VDIM :] = gathered[pairs:]
    left = lhs[...].astype(BF16)
    columns_all = wout.shape[1]
    width = columns_all // nh

    def mate_copy(chip, block):
        return pltpu.make_async_remote_copy(
            src_ref=blocks.at[block],
            dst_ref=pair_in.at[chip],
            send_sem=p_send.at[chip],
            recv_sem=p_recv.at[chip],
            device_id={"head": mate},
            device_id_type=MESH,
        )

    def chip_copy(chip, source):
        return pltpu.make_async_remote_copy(
            src_ref=chip_sum.at[chip],
            dst_ref=sums.at[source],
            send_sem=o_send.at[chip],
            recv_sem=o_recv.at[source],
            device_id={"head": 2 * chip + core},
            device_id_type=MESH,
        )

    def add_mate(chip):
        mate_copy(chip, 2 * chip).wait_recv()
        both = keep[2 * chip + core] + pair_in[chip].astype(F32)
        chip_sum[chip] = both.astype(BF16)

        @pl.when(x != chip)
        def _():
            chip_copy(chip, x).start()

        @pl.when(x == chip)
        def _():
            final[...] = both

    done = 0
    tile = 256
    for at in range(0, columns_all, tile):
        stop = min(at + tile, columns_all)
        part[:, at:stop] = dot(left, wout[:, at:stop])
        while done < nh and (done + 1) * width <= stop:
            start = done * width
            floor = start // 128 * 128
            ceil = min(-(-(start + width) // 128) * 128, columns_all)
            block = part[:, floor:ceil]
            if start > floor:
                block = pltpu.roll(block, ceil - start, 1)
            keep[done] = block[:, :width]
            blocks[done] = block[:, :width].astype(BF16)

            @pl.when(core != done % 2)
            def _(j=done):
                mate_copy(j // 2, j).start()

            if done % 2 == 1 and done > 1:
                add_mate(done // 2 - 1)
            done += 1
    add_mate(nx - 1)
    for d in range(1, ny):
        value_copy(d).wait_send()
    for chip in range(nx):
        mate_copy(chip, 2 * chip).wait_send()
    result = final[...]
    for d in range(1, nx):
        chip_copy(x_at[d], x_at[d]).wait_recv()
        result = result + sums[x_at[d]].astype(F32)
    final[...] = result
    for row in range(ny * samples):
        out_ref[row] = final[2 * row : 2 * row + 2, :]
    for d in range(1, nx):
        chip_copy(x_at[d], x).wait_send()


def shards(
    q_nope,
    q_rope,
    new_latent,
    new_rope,
    prompt_latent,
    prompt_rope,
    suffix_latent,
    suffix_rope,
    sample_prompt,
    suffix_len,
    w_uk,
    w_uv,
    w_out,
):
    nz, ny, nh = (lax.axis_size(name) for name in ("prompt", "sample", "head"))
    slots = nz * ny
    samples = q_nope.shape[0]
    pairs = 2 * samples
    heads = w_uk.shape[0]
    length = prompt_latent.shape[1]
    width = w_out.shape[1] // nh
    used = 2 * min(MOST, slots)
    rows_all = used * heads
    count = 16 * pairs
    vmem = pltpu.VMEM
    dma = pltpu.SemaphoreType.DMA
    in_vmem = pl.BlockSpec(memory_space=pltpu.VMEM)
    in_smem = pl.BlockSpec(memory_space=pltpu.SMEM)
    in_hbm = pl.BlockSpec(memory_space=pltpu.HBM)
    arrays = (
        q_nope,
        q_rope,
        new_latent,
        new_rope,
        prompt_latent,
        prompt_rope,
        suffix_latent,
        suffix_rope,
        w_uk,
        w_uv,
        w_out,
    )
    return pl.pallas_call(
        functools.partial(kernel, (nz, ny, nh)),
        out_shape=jax.ShapeDtypeStruct((samples * ny, 2, width), F32),
        in_specs=[in_smem] * 2 + [in_hbm] * 11,
        out_specs=in_vmem,
        scratch_shapes=[
            vmem(q_nope.shape, BF16),
            vmem(q_rope.shape, BF16),
            vmem(new_latent.shape, BF16),
            vmem(new_rope.shape, BF16),
            vmem(prompt_latent.shape[1:], BF16),
            vmem(prompt_rope.shape[1:], BF16),
            vmem(suffix_latent.shape, BF16),
            vmem(suffix_rope.shape, BF16),
            vmem(w_uk.shape, BF16),
            vmem(w_uv.shape, BF16),
            vmem(w_out.shape, BF16),
            vmem((pairs, heads * NOPE), F32),
            vmem((pairs, LAT + NOPE), F32),
            vmem((pairs * 2 * heads, NOPE), F32),
            vmem((samples + 1, 4 * heads, NOPE), BF16),
            vmem((slots, 4 * heads, NOPE), BF16),
            vmem((slots, 4 * heads, NOPE), BF16),
            vmem((slots * 4 * heads, NOPE), F32),
            vmem((LAT // 128, count, 128), F32),
            vmem((count, NOPE), F32),
            vmem((count, suffix_latent.shape[1]), F32),
            vmem((count, pairs), F32),
            vmem((count, VDIM), F32),
            vmem((LAT // 128, count, 128), F32),
            vmem((count, VDIM), F32),
            vmem((count, VDIM), F32),
            vmem((LAT // 128, rows_all, 128), F32),
            vmem((rows_all, NOPE), F32),
            vmem((rows_all, length), F32),
            vmem((rows_all, length), BF16),
            vmem((LAT // 128, rows_all, 128), F32),
            vmem((32 * slots, VDIM), F32),
            vmem((slots, 32, VDIM), BF16),
            vmem((slots, 32, VDIM), BF16),
            vmem((count, VDIM), F32),
            vmem((ny, 2 * pairs, heads * VDIM // 2), BF16),
            vmem((ny * pairs, heads * VDIM), F32),
            vmem((ny * pairs, w_out.shape[1]), F32),
            vmem((nh, ny * pairs, width), F32),
            vmem((nh, ny * pairs, width), BF16),
            vmem((nh // 2, ny * pairs, width), BF16),
            vmem((nh // 2, ny * pairs, width), BF16),
            vmem((nh // 2, ny * pairs, width), BF16),
            vmem((ny * pairs, width), F32),
            dma((len(arrays),)),
            pltpu.SemaphoreType.REGULAR,
            dma((slots,)),
            dma((slots,)),
            dma((slots,)),
            dma((slots,)),
            dma((ny,)),
            dma((ny,)),
            dma((nh // 2,)),
            dma((nh // 2,)),
            dma((nh // 2,)),
            dma((nh // 2,)),
        ],
        compiler_params=pltpu.CompilerParams(
            collective_id=0, has_side_effects=True, vmem_limit_bytes=56 * 1024 * 1024
        ),
        cost_estimate=pl.CostEstimate(
            flops=4 * 10**9, bytes_accessed=13 * 10**6, transcendentals=10**6
        ),
    )(sample_prompt, suffix_len, *arrays).astype(BF16)


def solution(mesh):
    placed = (
        P(("prompt", "sample"), None, "head"),
        P(("prompt", "sample"), None, "head"),
        P(("prompt", "sample"), None, None),
        P(("prompt", "sample"), None, None),
        P(("prompt", "sample"), None, None),
        P(("prompt", "sample"), None, None),
        P(("prompt", "sample"), None, None),
        P(("prompt", "sample"), None, None),
        P(("prompt", "sample")),
        P(("prompt", "sample")),
        P("head", None, None),
        P("head", None, None),
        P("head", "sample"),
    )
    return jax.shard_map(
        shards,
        mesh=mesh,
        in_specs=placed,
        out_specs=P("prompt", None, ("sample", "head")),
        check_vma=False,
    )
```

time: 52 us -> 54.9 us (1.056); the launches traced: 51.3 us -> 54.8 us
  Pallas kernels: 49.8 us -> 53.2 us
  other arithmetic: 0 us -> 1.55 us
  local copies, waits for them, and re-layouts: 1.45 us -> 0 us
    pallas_call x1, Pallas kernels: 49.8 us -> 53.2 us  [shards(): pl.pallas_call(functools.partial(kernel, (nz, ny, nh)), out_shape=jax.Sha...]
    convert_element_type x0 -> x1, other arithmetic: none -> 1.55 us  [shards(): return pl.pallas_call(functools.partial(kernel, (nz, ny, nh)), out_shape=...]
    reshape x1 -> x0, local copies, waits for them, and re-layouts: 1.45 us -> none  [shards(): return result.reshape(ny * samples, 2, width)]
where the time goes in v3:
time: 54.9 us; the launch traced here: 54.8 us
  Pallas kernels  53.2 us (97%)
  other arithmetic  1.55 us (3%)
    pallas_call x1, Pallas kernels, shards(): pl.pallas_call(functools.partial(kernel, (nz, ny, nh)), out_shape=jax.Sha...  53.2 us
    convert_element_type x1, other arithmetic, shards(): return pl.pallas_call(functools.partial(kernel, (nz, ny, nh)), out_shape=...  1.55 us

profile of v3, /device:TPU:1, one launch (start us, length us, event | category | flops | bytes accessed | tf_op | source)
XLA Modules:
  0.0 54.8 jit_solution(10045830952850482169)
XLA Ops:
  0.0 53.2 %shard_map.127 = f32[48,2,224]{2,1,0:T(2,128)} custom-call(s32[12]{0:T(128)} %sp_ref.1, s32[12]{0:T(128)} %len_ref.1, bf16[12,2,1536]{2,1,0:T(2,128)(2,1)} %q_hbm.1, bf16[12,2,768]{2,1,0:T(2,128)(2,1)} %r_hbm.1, bf16[12,2,512]{2,1,0:T(2,128)(2,1)} %nl_hbm.1, bf16[12,2,64]{2,1,0:T(2,128)(2,1)} %nr_hbm.1, bf16[1,2048,512]{2,1,0:T(8,128)(2,1)} %plat_hbm.1, ...), custom_call_target="tpu_custom_call" | custom-call | flops 4000000000 | bytes 13000000 | tf_op jit(solution)/shard_map/pallas_call | solution.py:559
  53.2 1.5 %convert_element_type.3 = bf16[48,2,224]{2,1,0:T(2,128)(2,1)} convert(f32[48,2,224]{2,1,0:T(2,128)} %shard_map.127) | non-fusion elementwise | flops 21504 | bytes 129024 | tf_op jit(solution)/shard_map/convert_element_type | solution.py:628

commit v4 on v1

v4 whole, which is shorter than its diff:
```python
import functools
import math

import jax
import jax.numpy as jnp
from jax import lax
from jax.experimental import pallas as pl
from jax.experimental.pallas import tpu as pltpu
from jax.sharding import PartitionSpec as P

NOPE = 128
ROPE = 64
LAT = 512
VDIM = 128
F32 = jnp.float32
BF16 = jnp.bfloat16
MESH = pl.DeviceIdType.MESH
FLOOR = -1e30
SCALE = 1.0 / math.sqrt(NOPE + ROPE)
EXP2_SCALE = SCALE * math.log2(math.e)
CHUNKS = 2
NT = (((1,), (1,)), ((), ()))


def dot(left, right):
    return jnp.dot(left, right, preferred_element_type=F32)


def dot_nt(left, right):
    return lax.dot_general(left, right, NT, preferred_element_type=F32)


def put(ref, first, count, stride, value):
    for tile in range(ref.shape[0]):
        ref[tile, pl.ds(first, count, stride=stride), :] = value[:, 128 * tile : 128 * (tile + 1)]


def take(ref, first, count, stride):
    tiles = [ref[tile, pl.ds(first, count, stride=stride), :] for tile in range(ref.shape[0])]
    return jnp.concatenate(tiles, axis=1)


def whole(ref, rows=slice(None)):
    return jnp.concatenate([ref[tile, rows, :] for tile in range(ref.shape[0])], axis=1)


def fill(ref, value, rows=slice(None)):
    for tile in range(ref.shape[0]):
        ref[tile, rows, :] = value[:, 128 * tile : 128 * (tile + 1)]


def iota(shape, axis):
    return lax.broadcasted_iota(jnp.int32, shape, axis)


def kernel(
    sizes,
    sp_ref,
    len_ref,
    q_hbm,
    r_hbm,
    nl_hbm,
    nr_hbm,
    plat_hbm,
    prope_hbm,
    slat_hbm,
    srope_hbm,
    wuk_hbm,
    wuv_hbm,
    wout_hbm,
    out_ref,
    q_ref,
    r_ref,
    nl_ref,
    nr_ref,
    plat,
    prope,
    slat,
    srope,
    wuk,
    wuv,
    wout,
    tok,
    ntok,
    qf,
    qb,
    sb,
    rb,
    xf,
    lqf,
    lrf,
    lsc,
    lnew,
    linv,
    lof,
    lvf,
    lse_col,
    plf,
    prf,
    sc,
    pb,
    pof,
    rvf,
    back,
    rr,
    cf,
    vg0,
    vg1,
    lhs0,
    lhs1,
    part,
    keep0,
    keep1,
    blocks0,
    blocks1,
    pair_in0,
    pair_in1,
    chip_sum0,
    chip_sum1,
    sums0,
    sums1,
    final0,
    final1,
    load_sem,
    q_send,
    q_recv,
    b_send,
    b_recv,
    v_send,
    v_recv,
    p_send,
    p_recv,
    o_send,
    o_recv,
):
    nz, ny, nh = sizes
    nx = nh // 2
    slots = nz * ny
    samples = q_ref.shape[0]
    pairs = 2 * samples
    heads = wuk.shape[0]
    wide = 2 * heads
    z = lax.axis_index("prompt")
    y = lax.axis_index("sample")
    head = lax.axis_index("head")
    core = lax.rem(head, 2)
    x = head // 2
    here = z * ny + y
    y_at = [lax.rem(y + d, ny) for d in range(ny)]
    x_at = [lax.rem(x + d, nx) for d in range(nx)]
    mate = head + 1 - 2 * core

    def ahead(k):
        step = k // ny
        half = (step + 1) // 2
        shift = jnp.where(step % 2 == 1, half, nz - half)
        return lax.rem(z + shift, nz), lax.rem(y + k % ny, ny)

    def behind(k):
        step = k // ny
        half = (step + 1) // 2
        shift = jnp.where(step % 2 == 1, nz - half, half)
        return lax.rem(z + shift, nz), lax.rem(y + ny - k % ny, ny)

    barrier = pltpu.get_barrier_semaphore()

    @pl.loop(1, slots)
    def _(k):
        to_z, to_y = ahead(k)
        pl.semaphore_signal(
            barrier, inc=1, device_id={"prompt": to_z, "sample": to_y}, device_id_type=MESH
        )

    near = [mate] + [2 * x_at[d] + core for d in range(1, nx)]
    for peer in near:
        pl.semaphore_signal(barrier, inc=1, device_id={"head": peer}, device_id_type=MESH)

    loads = [
        pltpu.make_async_copy(source, target, load_sem.at[index])
        for index, (source, target) in enumerate(
            (
                (q_hbm, q_ref),
                (r_hbm, r_ref),
                (nl_hbm, nl_ref),
                (nr_hbm, nr_ref),
                (wuk_hbm, wuk),
                (slat_hbm, slat),
                (srope_hbm, srope),
                (plat_hbm.at[0], plat),
                (prope_hbm.at[0], prope),
                (wuv_hbm, wuv),
                (wout_hbm, wout),
            )
        )
    ]
    for load in loads:
        load.start()

    loads[0].wait()
    for s in range(samples):
        tok[2 * s : 2 * s + 2, :] = q_ref[s].astype(F32)
    for h in range(heads):
        qf[pl.ds(h, pairs, stride=wide), :] = tok[:, h * NOPE : (h + 1) * NOPE]
    loads[1].wait()
    for s in range(samples):
        tok[2 * s : 2 * s + 2, : heads * ROPE] = r_ref[s].astype(F32)
    low = iota((pairs, NOPE), 1) < ROPE
    for h in range(heads):
        both = tok[:, h // 2 * NOPE : (h // 2 + 1) * NOPE]
        if h % 2 == 1:
            both = pltpu.roll(both, ROPE, 1)
        qf[pl.ds(heads + h, pairs, stride=wide), :] = jnp.where(low, both, 0.0)
    for s in range(samples):
        qb[s] = qf[2 * wide * s : 2 * wide * (s + 1), :].astype(BF16)

    pl.semaphore_wait(barrier, slots - 1 + len(near))

    def query_copy(k):
        to_z, to_y = ahead(k)
        return pltpu.make_async_remote_copy(
            src_ref=sb.at[k],
            dst_ref=rb.at[k],
            send_sem=q_send.at[k],
            recv_sem=q_recv.at[k],
            device_id={"prompt": to_z, "sample": to_y},
            device_id_type=MESH,
        )

    names = [sp_ref[s] for s in range(samples)]

    def sample_for(owner):
        found = 0
        for s in range(samples):
            found = jnp.where(names[s] == owner, s, found)
        return found

    @pl.loop(1, slots)
    def _(k):
        to_z, to_y = ahead(k)
        sb[k] = qb[sample_for(to_z * ny + to_y)]
        query_copy(k).start()

    rb[0] = qb[sample_for(here)]

    loads[2].wait()
    loads[3].wait()
    for s in range(samples):
        ntok[2 * s : 2 * s + 2, :LAT] = nl_ref[s].astype(F32)
        ntok[2 * s : 2 * s + 2, LAT:] = jnp.zeros((2, NOPE), F32)
        ntok[2 * s : 2 * s + 2, LAT : LAT + ROPE] = nr_ref[s].astype(F32)
    for h in range(heads, 16):
        lrf[pl.ds(h, pairs, stride=16), :] = jnp.zeros((pairs, NOPE), F32)
        put(lqf, h, pairs, 16, jnp.zeros((pairs, LAT), F32))
    loads[4].wait()
    for h in range(heads):
        rows = qf[pl.ds(h, pairs, stride=wide), :].astype(BF16)
        put(lqf, h, pairs, 16, dot(rows, wuk[h]))
        lrf[pl.ds(h, pairs, stride=16), :] = qf[pl.ds(heads + h, pairs, stride=wide), :]
    loads[5].wait()
    loads[6].wait()
    lane = iota((32, 128), 1)
    for s in range(samples):
        rows = slice(32 * s, 32 * s + 32)
        scores = dot_nt(whole(lqf, rows).astype(BF16), slat[s]) + dot(
            lrf[rows, :].astype(BF16)[:, :ROPE], srope[s]
        )
        lsc[rows, :] = jnp.where(lane < len_ref[s], scores, FLOOR)
    new_latent = ntok[:, :LAT].astype(BF16)
    new_rope = ntok[:, LAT:].astype(BF16)
    count = 16 * pairs
    new_scores = dot_nt(whole(lqf).astype(BF16), new_latent) + dot_nt(
        lrf[...].astype(BF16), new_rope
    )
    row, key = iota((count, pairs), 0), iota((count, pairs), 1)
    valid = ((key >> 1) == (row >> 5)) & ((key & 1) <= ((row >> 4) & 1))
    new_scores = jnp.where(valid, new_scores, FLOOR)
    old_scores = lsc[...]
    peak = jnp.maximum(
        jnp.max(old_scores, axis=1, keepdims=True), jnp.max(new_scores, axis=1, keepdims=True)
    )
    old_exp = jnp.exp2((old_scores - peak) * EXP2_SCALE)
    new_exp = jnp.exp2((new_scores - peak) * EXP2_SCALE)
    total = jnp.sum(old_exp, axis=1, keepdims=True) + jnp.sum(new_exp, axis=1, keepdims=True)
    lse_col[...] = jnp.broadcast_to(peak * SCALE + jnp.log(total), lse_col.shape)
    linv[...] = jnp.broadcast_to(1.0 / total, linv.shape)
    lsc[...] = old_exp
    lnew[...] = new_exp

    for load in loads[7:10]:
        load.wait()
    size = slots // CHUNKS
    duo = 2 * size
    rows_all = wide * size
    for h in range(heads, 16):
        rvf[pl.ds(h, duo, stride=16), :] = jnp.zeros((duo, VDIM), F32)

    def back_copy(k):
        to_z, to_y = behind(k)
        return pltpu.make_async_remote_copy(
            src_ref=back.at[k],
            dst_ref=rr.at[here],
            send_sem=b_send.at[k],
            recv_sem=b_recv.at[k],
            device_id={"prompt": to_z, "sample": to_y},
            device_id_type=MESH,
        )

    @pl.loop(0, CHUNKS)
    def _(chunk):
        base = chunk * size

        @pl.loop(0, size)
        def _(i):
            @pl.when(base + i > 0)
            def _():
                query_copy(base + i).wait_recv()

        xf[...] = rb[pl.ds(base, size)].astype(F32).reshape(xf.shape)
        for h in range(heads):
            rows = xf[pl.ds(h, duo, stride=wide), :].astype(BF16)
            put(plf, h, duo, heads, dot(rows, wuk[h]))
            prf[pl.ds(h, duo, stride=heads), :] = xf[pl.ds(heads + h, duo, stride=wide), :]
        lat_rows = whole(plf).astype(BF16)
        rope_rows = prf[...].astype(BF16)[:, :ROPE]
        length = plat.shape[0]
        tile = min(512, length)
        top = None
        for at in range(0, length, tile):
            scores = dot_nt(lat_rows, plat[at : at + tile, :]) + dot(
                rope_rows, prope[:, at : at + tile]
            )
            sc[:, at : at + tile] = scores
            for lanes in range(0, tile, 128):
                piece = scores[:, lanes : lanes + 128]
                top = piece if top is None else jnp.maximum(top, piece)
        peak = jnp.max(top, axis=1, keepdims=True)
        sums_of = jnp.zeros((rows_all, 128), F32)
        for at in range(0, length, tile):
            probs = jnp.exp2((sc[:, at : at + tile] - peak) * EXP2_SCALE)
            for lanes in range(0, tile, 128):
                sums_of = sums_of + probs[:, lanes : lanes + 128]
            pb[:, at : at + tile] = probs.astype(BF16)
        total = jnp.sum(sums_of, axis=1, keepdims=True)
        fill(pof, dot(pb[...], plat[...]) * (1.0 / total))
        for h in range(heads):
            rows = take(pof, h, duo, heads).astype(BF16)
            rvf[pl.ds(h, duo, stride=16), :] = dot(rows, wuv[h])
        lse = peak * SCALE + jnp.log(total)
        first = lse.astype(BF16).astype(F32)
        second = (lse - first).astype(BF16).astype(F32)
        third = lse - first - second
        row, lane = iota((rows_all, 128), 0), iota((rows_all, 128), 1)
        place = row - heads * ((row * 43691) >> 19)
        spread = (
            jnp.where(lane == place, first, 0.0)
            + jnp.where(lane == place + 16, second, 0.0)
            + jnp.where(lane == place + 32, third, 0.0)
        ).astype(BF16)
        at, of = iota((duo, rows_all), 0) * heads, iota((duo, rows_all), 1)
        pick = jnp.where((of >= at) & (of < at + heads), 1.0, 0.0).astype(BF16)
        rvf[pl.ds(heads, duo, stride=16), :] = dot(pick, spread)
        back[pl.ds(base, size)] = rvf[...].reshape(size, 32, VDIM).astype(BF16)

        @pl.loop(0, size)
        def _(i):
            @pl.when(base + i > 0)
            def _():
                back_copy(base + i).start()

    rr[here] = back[0]

    new_out = dot(lnew[...].astype(BF16), ntok[:, :LAT].astype(BF16))
    for s in range(samples):
        rows = slice(32 * s, 32 * s + 32)
        own_out = new_out[rows] + dot(lsc[rows, :].astype(BF16), slat[s])
        fill(lof, own_out * linv[rows, :1], rows)
    for h in range(heads):
        lvf[pl.ds(h, pairs, stride=16), :] = dot(take(lof, h, pairs, 16).astype(BF16), wuv[h])
    for h in range(heads, 16):
        lvf[pl.ds(h, pairs, stride=16), :] = jnp.zeros((pairs, VDIM), F32)
    @pl.loop(1, slots)
    def _(k):
        query_copy(k).wait_send()

    loads[10].wait()

    @pl.loop(1, slots)
    def _(k):
        back_copy(k).wait_recv()

    cuts = (0, 2 * pairs // 3, pairs)
    vgs = (vg0, vg1)
    lhss = (lhs0, lhs1)
    keeps = (keep0, keep1)
    blockss = (blocks0, blocks1)
    pair_ins = (pair_in0, pair_in1)
    chip_sums = (chip_sum0, chip_sum1)
    sumss = (sums0, sums1)
    finals = (final0, final1)

    def value_copy(g, d):
        return pltpu.make_async_remote_copy(
            src_ref=vgs[g].at[y],
            dst_ref=vgs[g].at[y],
            send_sem=v_send.at[g, d],
            recv_sem=v_recv.at[g, d],
            device_id={"sample": y_at[d]},
            device_id_type=MESH,
        )

    for s in range(samples):
        cf[32 * s : 32 * s + 32, :] = rr[names[s]].astype(F32)
    row, lane = iota((16, 128), 0), iota((16, 128), 1)
    mine = (lane == row) | (lane == row + 16) | (lane == row + 32)
    for g in range(2):
        for pair in range(cuts[g], cuts[g + 1]):
            rows = slice(16 * pair, 16 * pair + 16)
            stat = jnp.broadcast_to(cf[16 * pair + heads : 16 * pair + heads + 1, :], (16, 128))
            lse_prompt = jnp.sum(jnp.where(mine, stat, 0.0), axis=1, keepdims=True)
            lse_local = lse_col[rows, :]
            top = jnp.maximum(lse_prompt, lse_local)
            weight_prompt = jnp.exp(lse_prompt - top)
            weight_local = jnp.exp(lse_local - top)
            lvf[rows, :] = (weight_prompt * cf[rows, :] + weight_local * lvf[rows, :]) / (
                weight_prompt + weight_local
            )
        rows_of = cuts[g + 1] - cuts[g]
        columns = [
            lvf[pl.ds(16 * cuts[g] + h, rows_of, stride=16), :] for h in range(heads)
        ]
        folds = 16 // rows_of if rows_of < 16 else 1
        per = heads // folds
        vgs[g][y] = jnp.concatenate(
            [
                jnp.concatenate(columns[fold * per : (fold + 1) * per], axis=1)
                for fold in range(folds)
            ],
            axis=0,
        ).astype(BF16)
        for d in range(1, ny):
            value_copy(g, d).start()

    @pl.loop(1, slots)
    def _(k):
        back_copy(k).wait_send()

    columns_all = wout.shape[1]
    width = columns_all // nh

    def mate_copy(g, chip, block):
        return pltpu.make_async_remote_copy(
            src_ref=blockss[g].at[block],
            dst_ref=pair_ins[g].at[chip],
            send_sem=p_send.at[g, chip],
            recv_sem=p_recv.at[g, chip],
            device_id={"head": mate},
            device_id_type=MESH,
        )

    def chip_copy(g, chip, source):
        return pltpu.make_async_remote_copy(
            src_ref=chip_sums[g].at[chip],
            dst_ref=sumss[g].at[source],
            send_sem=o_send.at[g, chip],
            recv_sem=o_recv.at[g, source],
            device_id={"head": 2 * chip + core},
            device_id_type=MESH,
        )

    def add_mate(g, chip):
        mate_copy(g, chip, 2 * chip).wait_recv()
        both = keeps[g][2 * chip + core] + pair_ins[g][chip].astype(F32)
        chip_sums[g][chip] = both.astype(BF16)

        @pl.when(x != chip)
        def _():
            chip_copy(g, chip, x).start()

        @pl.when(x == chip)
        def _():
            finals[g][...] = both

    for g in range(2):
        rows_of = cuts[g + 1] - cuts[g]
        folds = 16 // rows_of if rows_of < 16 else 1
        inner = heads * VDIM // folds
        for d in range(1, ny):
            value_copy(g, d).wait_recv()
        for d in range(ny):
            gathered = vgs[g][d].astype(F32)
            for fold in range(folds):
                lhss[g][rows_of * d : rows_of * (d + 1), fold * inner : (fold + 1) * inner] = gathered[
                    fold * rows_of : (fold + 1) * rows_of
                ]
        left = lhss[g][...].astype(BF16)
        rows_here = slice(ny * cuts[g], ny * cuts[g + 1])
        done = 0
        tile = 256
        for at in range(0, columns_all, tile):
            stop = min(at + tile, columns_all)
            part[rows_here, at:stop] = dot(left, wout[:, at:stop])
            while done < nh and (done + 1) * width <= stop:
                start = done * width
                floor = start // 128 * 128
                ceil = min(-(-(start + width) // 128) * 128, columns_all)
                block = part[rows_here, floor:ceil]
                if start > floor:
                    block = pltpu.roll(block, ceil - start, 1)
                keeps[g][done] = block[:, :width]
                blockss[g][done] = block[:, :width].astype(BF16)

                @pl.when(core != done % 2)
                def _(j=done):
                    mate_copy(g, j // 2, j).start()

                if done % 2 == 1 and done > 1:
                    add_mate(g, done // 2 - 1)
                done += 1
        add_mate(g, nx - 1)

    for g in range(2):
        for d in range(1, ny):
            value_copy(g, d).wait_send()
        for chip in range(nx):
            mate_copy(g, chip, 2 * chip).wait_send()
    for g in range(2):
        result = finals[g][...]
        for d in range(1, nx):
            chip_copy(g, x_at[d], x_at[d]).wait_recv()
            result = result + sumss[g][x_at[d]].astype(F32)
        finals[g][...] = result
        rows_of = cuts[g + 1] - cuts[g]
        for d in range(ny):
            for s in range(rows_of // 2):
                out_ref[d * samples + cuts[g] // 2 + s] = finals[g][
                    rows_of * d + 2 * s : rows_of * d + 2 * s + 2, :
                ].astype(BF16)
    for g in range(2):
        for d in range(1, nx):
            chip_copy(g, x_at[d], x).wait_send()


def shards(
    q_nope,
    q_rope,
    new_latent,
    new_rope,
    prompt_latent,
    prompt_rope,
    suffix_latent,
    suffix_rope,
    sample_prompt,
    suffix_len,
    w_uk,
    w_uv,
    w_out,
):
    nz, ny, nh = (lax.axis_size(name) for name in ("prompt", "sample", "head"))
    slots = nz * ny
    samples = q_nope.shape[0]
    pairs = 2 * samples
    heads = w_uk.shape[0]
    length = prompt_latent.shape[1]
    width = w_out.shape[1] // nh
    size = slots // CHUNKS
    duo = 2 * size
    rows_all = duo * heads
    big = 2 * pairs // 3
    small = pairs - big
    fold = max(1, 16 // small)
    fold_big = max(1, 16 // big)
    count = 16 * pairs
    vmem = pltpu.VMEM
    dma = pltpu.SemaphoreType.DMA
    in_vmem = pl.BlockSpec(memory_space=pltpu.VMEM)
    in_smem = pl.BlockSpec(memory_space=pltpu.SMEM)
    in_hbm = pl.BlockSpec(memory_space=pltpu.HBM)
    arrays = (
        q_nope,
        q_rope,
        new_latent,
        new_rope,
        prompt_latent,
        prompt_rope,
        suffix_latent,
        suffix_rope,
        w_uk,
        w_uv,
        w_out,
    )
    return pl.pallas_call(
        functools.partial(kernel, (nz, ny, nh)),
        out_shape=jax.ShapeDtypeStruct((samples * ny, 2, width), BF16),
        in_specs=[in_smem] * 2 + [in_hbm] * 11,
        out_specs=in_vmem,
        scratch_shapes=[
            vmem(q_nope.shape, BF16),
            vmem(q_rope.shape, BF16),
            vmem(new_latent.shape, BF16),
            vmem(new_rope.shape, BF16),
            vmem(prompt_latent.shape[1:], BF16),
            vmem(prompt_rope.shape[1:], BF16),
            vmem(suffix_latent.shape, BF16),
            vmem(suffix_rope.shape, BF16),
            vmem(w_uk.shape, BF16),
            vmem(w_uv.shape, BF16),
            vmem(w_out.shape, BF16),
            vmem((pairs, heads * NOPE), F32),
            vmem((pairs, LAT + NOPE), F32),
            vmem((pairs * 2 * heads, NOPE), F32),
            vmem((samples, 4 * heads, NOPE), BF16),
            vmem((slots, 4 * heads, NOPE), BF16),
            vmem((slots, 4 * heads, NOPE), BF16),
            vmem((size * 4 * heads, NOPE), F32),
            vmem((LAT // 128, count, 128), F32),
            vmem((count, NOPE), F32),
            vmem((count, suffix_latent.shape[1]), F32),
            vmem((count, pairs), F32),
            vmem((count, VDIM), F32),
            vmem((LAT // 128, count, 128), F32),
            vmem((count, VDIM), F32),
            vmem((count, VDIM), F32),
            vmem((LAT // 128, rows_all, 128), F32),
            vmem((rows_all, NOPE), F32),
            vmem((rows_all, length), F32),
            vmem((rows_all, length), BF16),
            vmem((LAT // 128, rows_all, 128), F32),
            vmem((32 * size, VDIM), F32),
            vmem((slots, 32, VDIM), BF16),
            vmem((slots, 32, VDIM), BF16),
            vmem((count, VDIM), F32),
            vmem((ny, big * fold_big, heads * VDIM // fold_big), BF16),
            vmem((ny, small * fold, heads * VDIM // fold), BF16),
            vmem((ny * big, heads * VDIM), F32),
            vmem((ny * small, heads * VDIM), F32),
            vmem((ny * pairs, w_out.shape[1]), F32),
            vmem((nh, ny * big, width), F32),
            vmem((nh, ny * small, width), F32),
            vmem((nh, ny * big, width), BF16),
            vmem((nh, ny * small, width), BF16),
            vmem((nh // 2, ny * big, width), BF16),
            vmem((nh // 2, ny * small, width), BF16),
            vmem((nh // 2, ny * big, width), BF16),
            vmem((nh // 2, ny * small, width), BF16),
            vmem((nh // 2, ny * big, width), BF16),
            vmem((nh // 2, ny * small, width), BF16),
            vmem((ny * big, width), F32),
            vmem((ny * small, width), F32),
            dma((len(arrays),)),
            dma((slots,)),
            dma((slots,)),
            dma((slots,)),
            dma((slots,)),
            dma((2, ny)),
            dma((2, ny)),
            dma((2, nh // 2)),
            dma((2, nh // 2)),
            dma((2, nh // 2)),
            dma((2, nh // 2)),
        ],
        compiler_params=pltpu.CompilerParams(
            collective_id=0, has_side_effects=True, vmem_limit_bytes=56 * 1024 * 1024
        ),
        cost_estimate=pl.CostEstimate(
            flops=4 * 10**9, bytes_accessed=13 * 10**6, transcendentals=10**6
        ),
    )(sample_prompt, suffix_len, *arrays)


def solution(mesh):
    placed = (
        P(("prompt", "sample"), None, "head"),
        P(("prompt", "sample"), None, "head"),
        P(("prompt", "sample"), None, None),
        P(("prompt", "sample"), None, None),
        P(("prompt", "sample"), None, None),
        P(("prompt", "sample"), None, None),
        P(("prompt", "sample"), None, None),
        P(("prompt", "sample"), None, None),
        P(("prompt", "sample")),
        P(("prompt", "sample")),
        P("head", None, None),
        P("head", None, None),
        P("head", "sample"),
    )
    return jax.shard_map(
        shards,
        mesh=mesh,
        in_specs=placed,
        out_specs=P("prompt", None, ("sample", "head")),
        check_vma=False,
    )
```

time: 52 us -> 53.6 us (1.031)
  Pallas kernels: 49.8 us -> 51.8 us
    pallas_call x1, Pallas kernels: 49.8 us -> 51.8 us  [shards(): pl.pallas_call(functools.partial(kernel, (nz, ny, nh)), out_shape=jax.Sha...]
    unnamed x0 -> x1, local copies, waits for them, and re-layouts: none -> 1.45 us
    reshape x1 -> x0, local copies, waits for them, and re-layouts: 1.45 us -> none  [shards(): return result.reshape(ny * samples, 2, width)]
where the time goes in v4:
time: 53.6 us; the launch traced here: 53.2 us
  Pallas kernels  51.8 us (97%)
  local copies, waits for them, and re-layouts  1.45 us (3%)
    pallas_call x1, Pallas kernels, shards(): pl.pallas_call(functools.partial(kernel, (nz, ny, nh)), out_shape=jax.Sha...  51.8 us
    unnamed x1, local copies, waits for them, and re-layouts  1.45 us

profile of v4, /device:TPU:1, one launch (start us, length us, event | category | flops | bytes accessed | tf_op | source)
XLA Modules:
  0.0 53.2 jit_solution(4947695148699727095)
XLA Ops:
  0.0 51.8 %shard_map.127 = bf16[48,2,224]{2,1,0:T(2,128)(2,1)} custom-call(s32[12]{0:T(128)} %sp_ref.1, s32[12]{0:T(128)} %len_ref.1, bf16[12,2,1536]{2,1,0:T(2,128)(2,1)} %q_hbm.1, bf16[12,2,768]{2,1,0:T(2,128)(2,1)} %r_hbm.1, bf16[12,2,512]{2,1,0:T(2,128)(2,1)} %nl_hbm.1, bf16[12,2,64]{2,1,0:T(2,128)(2,1)} %nr_hbm.1, bf16[1,2048,512]{2,1,0:T(8,128)(2,1)} %plat_hbm.1, ...), custom_call_target="tpu_custom_call" | custom-call | flops 4000000000 | bytes 13000000 | tf_op jit(solution)/shard_map/pallas_call | solution.py:591
  51.8 1.5 %copy.15 = bf16[48,2,224]{2,1,0:T(2,128)(2,1)} copy(bf16[48,2,224]{2,1,0:T(2,128)(2,1)} %shard_map.127) | data formatting | bytes 86016

commit v5 on v1

--- a/solution.py
+++ b/solution.py
@@ -57,10 +57,10 @@
     sizes,
     sp_ref,
     len_ref,
-    q_ref,
-    r_ref,
-    nl_ref,
-    nr_ref,
+    q_hbm,
+    r_hbm,
+    nl_hbm,
+    nr_hbm,
     plat_hbm,
     prope_hbm,
     slat_hbm,
@@ -69,6 +69,10 @@
     wuv_hbm,
     wout_hbm,
     out_ref,
+    q_ref,
+    r_ref,
+    nl_ref,
+    nr_ref,
     plat,
     prope,
     slat,
@@ -86,6 +90,8 @@
     lqf,
     lrf,
     lsc,
+    lnew,
+    linv,
     lof,
     lvf,
     lse_col,
@@ -124,24 +130,6 @@
     head = lax.axis_index("head")
     here = z * ny + y
 
-    loads = [
-        pltpu.make_async_copy(source, target, load_sem.at[index])
-        for index, (source, target) in enumerate(
-            (
-                (wuk_hbm, wuk),
-                (slat_hbm, slat),
-                (srope_hbm, srope),
-                (wuv_hbm, wuv),
-                (plat_hbm.at[0], plat),
-                (prope_hbm.at[0], prope),
-                (wout_hbm, wout),
-            )
-        )
-    ]
-    for load in loads:
-        load.start()
-    load_wuk, load_slat, load_srope, load_wuv, load_plat, load_prope, load_wout = loads
-
     def ahead(k):
         step = k // ny
         half = (step + 1) // 2
@@ -154,6 +142,26 @@
         shift = jnp.where(step % 2 == 1, nz - half, half)
         return lax.rem(z + shift, nz), lax.rem(y + ny - k % ny, ny)
 
+    loads = [
+        pltpu.make_async_copy(source, target, load_sem.at[index])
+        for index, (source, target) in enumerate(
+            (
+                (q_hbm, q_ref),
+                (r_hbm, r_ref),
+                (nl_hbm, nl_ref),
+                (nr_hbm, nr_ref),
+                (wuk_hbm, wuk),
+                (slat_hbm, slat),
+                (srope_hbm, srope),
+                (plat_hbm.at[0], plat),
+                (prope_hbm.at[0], prope),
+                (wuv_hbm, wuv),
+                (wout_hbm, wout),
+            )
+        )
+    ]
+    for load in loads[:2]:
+        load.start()
     barrier = pltpu.get_barrier_semaphore()
 
     @pl.loop(1, slots)
@@ -169,13 +177,15 @@
             barrier, inc=1, device_id={"head": lax.rem(head + d, nh)}, device_id_type=MESH
         )
 
+    for load in loads[2:]:
+        load.start()
+
+    loads[0].wait()
     for s in range(samples):
         tok[2 * s : 2 * s + 2, :] = q_ref[s].astype(F32)
-        ntok[2 * s : 2 * s + 2, :LAT] = nl_ref[s].astype(F32)
-        ntok[2 * s : 2 * s + 2, LAT:] = jnp.zeros((2, NOPE), F32)
-        ntok[2 * s : 2 * s + 2, LAT : LAT + ROPE] = nr_ref[s].astype(F32)
     for h in range(heads):
         qf[pl.ds(h, pairs, stride=wide), :] = tok[:, h * NOPE : (h + 1) * NOPE]
+    loads[1].wait()
     for s in range(samples):
         tok[2 * s : 2 * s + 2, : heads * ROPE] = r_ref[s].astype(F32)
     low = iota((pairs, NOPE), 1) < ROPE
@@ -183,12 +193,7 @@
         both = tok[:, h // 2 * NOPE : (h // 2 + 1) * NOPE]
         if h % 2 == 1:
             both = pltpu.roll(both, ROPE, 1)
-        rope_rows = jnp.where(low, both, 0.0)
-        qf[pl.ds(heads + h, pairs, stride=wide), :] = rope_rows
-        lrf[pl.ds(h, pairs, stride=16), :] = rope_rows
-    for h in range(heads, 16):
-        lrf[pl.ds(h, pairs, stride=16), :] = jnp.zeros((pairs, NOPE), F32)
-        put(lqf, h, pairs, 16, jnp.zeros((pairs, LAT), F32))
+        qf[pl.ds(heads + h, pairs, stride=wide), :] = jnp.where(low, both, 0.0)
     for s in range(samples):
         qb[s] = qf[2 * wide * s : 2 * wide * (s + 1), :].astype(BF16)
 
@@ -205,13 +210,13 @@
             device_id_type=MESH,
         )
 
+    names = [sp_ref[s] for s in range(samples)]
+
     def sample_for(owner):
         found = 0
         for s in range(samples):
-            found = jnp.where(sp_ref[s] == owner, s, found)
+            found = jnp.where(names[s] == owner, s, found)
         return found
-
-    rb[0] = qb[sample_for(here)]
 
     @pl.loop(1, slots)
     def _(k):
@@ -219,19 +224,31 @@
         sb[k] = qb[sample_for(to_z * ny + to_y)]
         query_copy(k).start()
 
-    load_wuk.wait()
+    rb[0] = qb[sample_for(here)]
+
+    loads[2].wait()
+    loads[3].wait()
+    for s in range(samples):
+        ntok[2 * s : 2 * s + 2, :LAT] = nl_ref[s].astype(F32)
+        ntok[2 * s : 2 * s + 2, LAT:] = jnp.zeros((2, NOPE), F32)
+        ntok[2 * s : 2 * s + 2, LAT : LAT + ROPE] = nr_ref[s].astype(F32)
+    for h in range(heads, 16):
+        lrf[pl.ds(h, pairs, stride=16), :] = jnp.zeros((pairs, NOPE), F32)
+        put(lqf, h, pairs, 16, jnp.zeros((pairs, LAT), F32))
+    loads[4].wait()
     for h in range(heads):
         rows = qf[pl.ds(h, pairs, stride=wide), :].astype(BF16)
         put(lqf, h, pairs, 16, dot(rows, wuk[h]))
-    load_slat.wait()
-    load_srope.wait()
+        lrf[pl.ds(h, pairs, stride=16), :] = qf[pl.ds(heads + h, pairs, stride=wide), :]
+    loads[5].wait()
+    loads[6].wait()
     lane = iota((32, 128), 1)
     for s in range(samples):
         rows = slice(32 * s, 32 * s + 32)
-        part_scores = dot_nt(whole(lqf, rows).astype(BF16), slat[s]) + dot(
+        scores = dot_nt(whole(lqf, rows).astype(BF16), slat[s]) + dot(
             lrf[rows, :].astype(BF16)[:, :ROPE], srope[s]
         )
-        lsc[rows, :] = jnp.where(lane < len_ref[s], part_scores, FLOOR)
+        lsc[rows, :] = jnp.where(lane < len_ref[s], scores, FLOOR)
     new_latent = ntok[:, :LAT].astype(BF16)
     new_rope = ntok[:, LAT:].astype(BF16)
     count = 16 * pairs
@@ -249,22 +266,12 @@
     new_exp = jnp.exp2((new_scores - peak) * EXP2_SCALE)
     total = jnp.sum(old_exp, axis=1, keepdims=True) + jnp.sum(new_exp, axis=1, keepdims=True)
     lse_col[...] = jnp.broadcast_to(peak * SCALE + jnp.log(total), lse_col.shape)
+    linv[...] = jnp.broadcast_to(1.0 / total, linv.shape)
     lsc[...] = old_exp
-    new_out = dot(new_exp.astype(BF16), new_latent)
-    inverse = 1.0 / total
-    for s in range(samples):
-        rows = slice(32 * s, 32 * s + 32)
-        own_out = new_out[rows] + dot(lsc[rows, :].astype(BF16), slat[s])
-        fill(lof, own_out * inverse[rows], rows)
-    load_wuv.wait()
-    for h in range(heads):
-        rows = take(lof, h, pairs, 16).astype(BF16)
-        lvf[pl.ds(h, pairs, stride=16), :] = dot(rows, wuv[h])
-    for h in range(heads, 16):
-        lvf[pl.ds(h, pairs, stride=16), :] = jnp.zeros((pairs, VDIM), F32)
-
-    load_plat.wait()
-    load_prope.wait()
+    lnew[...] = new_exp
+
+    for load in loads[7:10]:
+        load.wait()
     size = slots // CHUNKS
     duo = 2 * size
     rows_all = wide * size
@@ -301,19 +308,23 @@
         rope_rows = prf[...].astype(BF16)[:, :ROPE]
         length = plat.shape[0]
         tile = min(512, length)
-        peak = None
+        top = None
         for at in range(0, length, tile):
             scores = dot_nt(lat_rows, plat[at : at + tile, :]) + dot(
                 rope_rows, prope[:, at : at + tile]
             )
             sc[:, at : at + tile] = scores
-            top = jnp.max(scores, axis=1, keepdims=True)
-            peak = top if peak is None else jnp.maximum(peak, top)
-        total = jnp.zeros_like(peak)
+            for lanes in range(0, tile, 128):
+                piece = scores[:, lanes : lanes + 128]
+                top = piece if top is None else jnp.maximum(top, piece)
+        peak = jnp.max(top, axis=1, keepdims=True)
+        sums_of = jnp.zeros((rows_all, 128), F32)
         for at in range(0, length, tile):
             probs = jnp.exp2((sc[:, at : at + tile] - peak) * EXP2_SCALE)
-            total = total + jnp.sum(probs, axis=1, keepdims=True)
+            for lanes in range(0, tile, 128):
+                sums_of = sums_of + probs[:, lanes : lanes + 128]
             pb[:, at : at + tile] = probs.astype(BF16)
+        total = jnp.sum(sums_of, axis=1, keepdims=True)
         fill(pof, dot(pb[...], plat[...]) * (1.0 / total))
         for h in range(heads):
             rows = take(pof, h, duo, heads).astype(BF16)
@@ -342,6 +353,21 @@
 
     rr[here] = back[0]
 
+    new_out = dot(lnew[...].astype(BF16), ntok[:, :LAT].astype(BF16))
+    for s in range(samples):
+        rows = slice(32 * s, 32 * s + 32)
+        own_out = new_out[rows] + dot(lsc[rows, :].astype(BF16), slat[s])
+        fill(lof, own_out * linv[rows, :1], rows)
+    for h in range(heads):
+        lvf[pl.ds(h, pairs, stride=16), :] = dot(take(lof, h, pairs, 16).astype(BF16), wuv[h])
+    for h in range(heads, 16):
+        lvf[pl.ds(h, pairs, stride=16), :] = jnp.zeros((pairs, VDIM), F32)
+    @pl.loop(1, slots)
+    def _(k):
+        query_copy(k).wait_send()
+
+    loads[10].wait()
+
     @pl.loop(1, slots)
     def _(k):
         back_copy(k).wait_recv()
@@ -382,7 +408,6 @@
 
     for d in range(1, ny):
         value_copy(d).start()
-    load_wout.wait()
     for d in range(1, ny):
         value_copy(d).wait_recv()
 
@@ -412,7 +437,7 @@
         while done < nh and (done + 1) * width <= stop:
             start = done * width
             floor = start // 128 * 128
-            ceil = -(-(start + width) // 128) * 128
+            ceil = min(-(-(start + width) // 128) * 128, columns_all)
             block = part[:, floor:ceil]
             if start > floor:
                 block = pltpu.roll(block, ceil - start, 1)
@@ -423,6 +448,12 @@
                 sum_copy(j).start()
 
             done += 1
+    @pl.loop(1, slots)
+    def _(k):
+        back_copy(k).wait_send()
+
+    for d in range(1, ny):
+        value_copy(d).wait_send()
     result = blocks[head].astype(F32)
     for d in range(1, nh):
         source = lax.rem(head + d, nh)
@@ -437,13 +468,6 @@
         result = result + sums[source].astype(F32)
     out_ref[...] = result.astype(BF16)
 
-    @pl.loop(1, slots)
-    def _(k):
-        query_copy(k).wait_send()
-        back_copy(k).wait_send()
-
-    for d in range(1, ny):
-        value_copy(d).wait_send()
 
     @pl.loop(1, nh)
     def _(d):
@@ -474,19 +498,36 @@
     width = w_out.shape[1] // nh
     size = slots // CHUNKS
     duo = 2 * size
-    rows_all = 2 * heads * size
+    rows_all = duo * heads
     count = 16 * pairs
     vmem = pltpu.VMEM
     dma = pltpu.SemaphoreType.DMA
     in_vmem = pl.BlockSpec(memory_space=pltpu.VMEM)
     in_smem = pl.BlockSpec(memory_space=pltpu.SMEM)
-    in_hbm = pl.BlockSpec(memory_space=pl.ANY)
+    in_hbm = pl.BlockSpec(memory_space=pltpu.HBM)
+    arrays = (
+        q_nope,
+        q_rope,
+        new_latent,
+        new_rope,
+        prompt_latent,
+        prompt_rope,
+        suffix_latent,
+        suffix_rope,
+        w_uk,
+        w_uv,
+        w_out,
+    )
     result = pl.pallas_call(
         functools.partial(kernel, (nz, ny, nh)),
-        out_shape=jax.ShapeDtypeStruct((pairs * ny, width), BF16),
-        in_specs=[in_smem] * 2 + [in_vmem] * 4 + [in_hbm] * 7,
+        out_shape=jax.ShapeDtypeStruct((ny * pairs, width), BF16),
+        in_specs=[in_smem] * 2 + [in_hbm] * 11,
         out_specs=in_vmem,
         scratch_shapes=[
+            vmem(q_nope.shape, BF16),
+            vmem(q_rope.shape, BF16),
+            vmem(new_latent.shape, BF16),
+            vmem(new_rope.shape, BF16),
             vmem(prompt_latent.shape[1:], BF16),
             vmem(prompt_rope.shape[1:], BF16),
             vmem(suffix_latent.shape, BF16),
@@ -504,6 +545,8 @@
             vmem((LAT // 128, count, 128), F32),
             vmem((count, NOPE), F32),
             vmem((count, suffix_latent.shape[1]), F32),
+            vmem((count, pairs), F32),
+            vmem((count, VDIM), F32),
             vmem((LAT // 128, count, 128), F32),
             vmem((count, VDIM), F32),
             vmem((count, VDIM), F32),
@@ -512,7 +555,7 @@
             vmem((rows_all, length), F32),
             vmem((rows_all, length), BF16),
             vmem((LAT // 128, rows_all, 128), F32),
-            vmem((16 * duo, VDIM), F32),
+            vmem((32 * size, VDIM), F32),
             vmem((slots, 32, VDIM), BF16),
             vmem((slots, 32, VDIM), BF16),
             vmem((count, VDIM), F32),
@@ -521,7 +564,7 @@
             vmem((ny * pairs, w_out.shape[1]), F32),
             vmem((nh, ny * pairs, width), BF16),
             vmem((nh, ny * pairs, width), BF16),
-            dma((7,)),
+            dma((len(arrays),)),
             dma((slots,)),
             dma((slots,)),
             dma((slots,)),
@@ -535,23 +578,9 @@
             collective_id=0, has_side_effects=True, vmem_limit_bytes=56 * 1024 * 1024
         ),
         cost_estimate=pl.CostEstimate(
-            flops=5 * 10**9, bytes_accessed=13 * 10**6, transcendentals=2 * 10**6
+            flops=4 * 10**9, bytes_accessed=13 * 10**6, transcendentals=10**6
         ),
-    )(
-        sample_prompt,
-        suffix_len,
-        q_nope,
-        q_rope,
-        new_latent,
-        new_rope,
-        prompt_latent,
-        prompt_rope,
-        suffix_latent,
-        suffix_rope,
-        w_uk,
-        w_uv,
-        w_out,
-    )
+    )(sample_prompt, suffix_len, *arrays)
     return result.reshape(ny * samples, 2, width)
 
 

time: 52 us -> 51.7 us (level)
  no operation moved by 1% of the time
where the time goes in v5:
time: 51.7 us; the launch traced here: 50.9 us
  Pallas kernels  49.5 us (96%)
  local copies, waits for them, and re-layouts  1.45 us (3%)
    pallas_call x1, Pallas kernels, shards(): pl.pallas_call(functools.partial(kernel, (nz, ny, nh)), out_shape=jax.Sha...  49.5 us
    reshape x1, local copies, waits for them, and re-layouts, shards(): return result.reshape(ny * samples, 2, width)  1.45 us

profile of v5, /device:TPU:1, one launch (start us, length us, event | category | flops | bytes accessed | tf_op | source)
XLA Modules:
  0.0 50.9 jit_solution(5507456388780490090)
XLA Ops:
  0.0 49.5 %shard_map.127 = bf16[96,224]{1,0:T(8,128)(2,1)} custom-call(s32[12]{0:T(128)} %sp_ref.1, s32[12]{0:T(128)} %len_ref.1, bf16[12,2,1536]{2,1,0:T(2,128)(2,1)} %q_hbm.1, bf16[12,2,768]{2,1,0:T(2,128)(2,1)} %r_hbm.1, bf16[12,2,512]{2,1,0:T(2,128)(2,1)} %nl_hbm.1, bf16[12,2,64]{2,1,0:T(2,128)(2,1)} %nr_hbm.1, bf16[1,2048,512]{2,1,0:T(8,128)(2,1)} %plat_hbm.1, ...), custom_call_target="tpu_custom_call" | custom-call | flops 4000000000 | bytes 13000000 | tf_op jit(solution)/shard_map/pallas_call | solution.py:521
  49.5 1.5 %reshape.3 = bf16[48,2,224]{2,1,0:T(2,128)(2,1)} reshape(bf16[96,224]{1,0:T(8,128)(2,1)} %shard_map.127) | data formatting | bytes 86016 | tf_op jit(solution)/shard_map/reshape | solution.py:584

commit v6 on v4

--- a/solution.py
+++ b/solution.py
@@ -109,18 +109,10 @@
     lhs0,
     lhs1,
     part,
-    keep0,
-    keep1,
     blocks0,
     blocks1,
-    pair_in0,
-    pair_in1,
-    chip_sum0,
-    chip_sum1,
     sums0,
     sums1,
-    final0,
-    final1,
     load_sem,
     q_send,
     q_recv,
@@ -128,13 +120,10 @@
     b_recv,
     v_send,
     v_recv,
-    p_send,
-    p_recv,
     o_send,
     o_recv,
 ):
     nz, ny, nh = sizes
-    nx = nh // 2
     slots = nz * ny
     samples = q_ref.shape[0]
     pairs = 2 * samples
@@ -143,37 +132,24 @@
     z = lax.axis_index("prompt")
     y = lax.axis_index("sample")
     head = lax.axis_index("head")
-    core = lax.rem(head, 2)
-    x = head // 2
     here = z * ny + y
     y_at = [lax.rem(y + d, ny) for d in range(ny)]
-    x_at = [lax.rem(x + d, nx) for d in range(nx)]
-    mate = head + 1 - 2 * core
+    own = slots - ny
+
+    def other(i):
+        return jnp.where(i <= own, i - 1, i)
 
     def ahead(k):
-        step = k // ny
+        step = nz - 1 - k // ny
         half = (step + 1) // 2
         shift = jnp.where(step % 2 == 1, half, nz - half)
         return lax.rem(z + shift, nz), lax.rem(y + k % ny, ny)
 
     def behind(k):
-        step = k // ny
+        step = nz - 1 - k // ny
         half = (step + 1) // 2
         shift = jnp.where(step % 2 == 1, nz - half, half)
         return lax.rem(z + shift, nz), lax.rem(y + ny - k % ny, ny)
-
-    barrier = pltpu.get_barrier_semaphore()
-
-    @pl.loop(1, slots)
-    def _(k):
-        to_z, to_y = ahead(k)
-        pl.semaphore_signal(
-            barrier, inc=1, device_id={"prompt": to_z, "sample": to_y}, device_id_type=MESH
-        )
-
-    near = [mate] + [2 * x_at[d] + core for d in range(1, nx)]
-    for peer in near:
-        pl.semaphore_signal(barrier, inc=1, device_id={"head": peer}, device_id_type=MESH)
 
     loads = [
         pltpu.make_async_copy(source, target, load_sem.at[index])
@@ -193,7 +169,24 @@
             )
         )
     ]
-    for load in loads:
+    for load in loads[:2]:
+        load.start()
+    barrier = pltpu.get_barrier_semaphore()
+
+    @pl.loop(1, slots)
+    def _(i):
+        to_z, to_y = ahead(other(i))
+        pl.semaphore_signal(
+            barrier, inc=1, device_id={"prompt": to_z, "sample": to_y}, device_id_type=MESH
+        )
+
+    @pl.loop(1, nh)
+    def _(d):
+        pl.semaphore_signal(
+            barrier, inc=1, device_id={"head": lax.rem(head + d, nh)}, device_id_type=MESH
+        )
+
+    for load in loads[2:]:
         load.start()
 
     loads[0].wait()
@@ -213,7 +206,7 @@
     for s in range(samples):
         qb[s] = qf[2 * wide * s : 2 * wide * (s + 1), :].astype(BF16)
 
-    pl.semaphore_wait(barrier, slots - 1 + len(near))
+    pl.semaphore_wait(barrier, slots - 1 + nh - 1)
 
     def query_copy(k):
         to_z, to_y = ahead(k)
@@ -235,12 +228,13 @@
         return found
 
     @pl.loop(1, slots)
-    def _(k):
+    def _(i):
+        k = other(i)
         to_z, to_y = ahead(k)
         sb[k] = qb[sample_for(to_z * ny + to_y)]
         query_copy(k).start()
 
-    rb[0] = qb[sample_for(here)]
+    rb[own] = qb[sample_for(here)]
 
     loads[2].wait()
     loads[3].wait()
@@ -311,7 +305,7 @@
 
         @pl.loop(0, size)
         def _(i):
-            @pl.when(base + i > 0)
+            @pl.when(base + i != own)
             def _():
                 query_copy(base + i).wait_recv()
 
@@ -363,11 +357,11 @@
 
         @pl.loop(0, size)
         def _(i):
-            @pl.when(base + i > 0)
+            @pl.when(base + i != own)
             def _():
                 back_copy(base + i).start()
 
-    rr[here] = back[0]
+    rr[here] = back[own]
 
     new_out = dot(lnew[...].astype(BF16), ntok[:, :LAT].astype(BF16))
     for s in range(samples):
@@ -379,24 +373,20 @@
     for h in range(heads, 16):
         lvf[pl.ds(h, pairs, stride=16), :] = jnp.zeros((pairs, VDIM), F32)
     @pl.loop(1, slots)
-    def _(k):
-        query_copy(k).wait_send()
+    def _(i):
+        query_copy(other(i)).wait_send()
 
     loads[10].wait()
 
     @pl.loop(1, slots)
-    def _(k):
-        back_copy(k).wait_recv()
+    def _(i):
+        back_copy(other(i)).wait_recv()
 
     cuts = (0, 2 * pairs // 3, pairs)
     vgs = (vg0, vg1)
     lhss = (lhs0, lhs1)
-    keeps = (keep0, keep1)
     blockss = (blocks0, blocks1)
-    pair_ins = (pair_in0, pair_in1)
-    chip_sums = (chip_sum0, chip_sum1)
     sumss = (sums0, sums1)
-    finals = (final0, final1)
 
     def value_copy(g, d):
         return pltpu.make_async_remote_copy(
@@ -437,48 +427,25 @@
             ],
             axis=0,
         ).astype(BF16)
-        for d in range(1, ny):
+        for d in sorted(range(1, ny), key=lambda d: abs(d - ny // 2)):
             value_copy(g, d).start()
 
     @pl.loop(1, slots)
-    def _(k):
-        back_copy(k).wait_send()
+    def _(i):
+        back_copy(other(i)).wait_send()
 
     columns_all = wout.shape[1]
     width = columns_all // nh
 
-    def mate_copy(g, chip, block):
+    def sum_copy(g, target, source):
         return pltpu.make_async_remote_copy(
-            src_ref=blockss[g].at[block],
-            dst_ref=pair_ins[g].at[chip],
-            send_sem=p_send.at[g, chip],
-            recv_sem=p_recv.at[g, chip],
-            device_id={"head": mate},
+            src_ref=blockss[g].at[target],
+            dst_ref=sumss[g].at[source],
+            send_sem=o_send.at[g, target],
+            recv_sem=o_recv.at[g, source],
+            device_id={"head": target},
             device_id_type=MESH,
         )
-
-    def chip_copy(g, chip, source):
-        return pltpu.make_async_remote_copy(
-            src_ref=chip_sums[g].at[chip],
-            dst_ref=sumss[g].at[source],
-            send_sem=o_send.at[g, chip],
-            recv_sem=o_recv.at[g, source],
-            device_id={"head": 2 * chip + core},
-            device_id_type=MESH,
-        )
-
-    def add_mate(g, chip):
-        mate_copy(g, chip, 2 * chip).wait_recv()
-        both = keeps[g][2 * chip + core] + pair_ins[g][chip].astype(F32)
-        chip_sums[g][chip] = both.astype(BF16)
-
-        @pl.when(x != chip)
-        def _():
-            chip_copy(g, chip, x).start()
-
-        @pl.when(x == chip)
-        def _():
-            finals[g][...] = both
 
     for g in range(2):
         rows_of = cuts[g + 1] - cuts[g]
@@ -506,38 +473,33 @@
                 block = part[rows_here, floor:ceil]
                 if start > floor:
                     block = pltpu.roll(block, ceil - start, 1)
-                keeps[g][done] = block[:, :width]
                 blockss[g][done] = block[:, :width].astype(BF16)
 
-                @pl.when(core != done % 2)
+                @pl.when(head != done)
                 def _(j=done):
-                    mate_copy(g, j // 2, j).start()
-
-                if done % 2 == 1 and done > 1:
-                    add_mate(g, done // 2 - 1)
+                    sum_copy(g, j, head).start()
+
                 done += 1
-        add_mate(g, nx - 1)
 
     for g in range(2):
         for d in range(1, ny):
             value_copy(g, d).wait_send()
-        for chip in range(nx):
-            mate_copy(g, chip, 2 * chip).wait_send()
     for g in range(2):
-        result = finals[g][...]
-        for d in range(1, nx):
-            chip_copy(g, x_at[d], x_at[d]).wait_recv()
-            result = result + sumss[g][x_at[d]].astype(F32)
-        finals[g][...] = result
         rows_of = cuts[g + 1] - cuts[g]
+        result = blockss[g][head].astype(F32)
+        for d in range(1, nh):
+            source = lax.rem(head + d, nh)
+            sum_copy(g, source, source).wait_recv()
+            result = result + sumss[g][source].astype(F32)
+        result = result.astype(BF16)
         for d in range(ny):
-            for s in range(rows_of // 2):
-                out_ref[d * samples + cuts[g] // 2 + s] = finals[g][
-                    rows_of * d + 2 * s : rows_of * d + 2 * s + 2, :
-                ].astype(BF16)
-    for g in range(2):
-        for d in range(1, nx):
-            chip_copy(g, x_at[d], x).wait_send()
+            at = pairs * d + cuts[g]
+            out_ref[at : at + rows_of, :] = result[rows_of * d : rows_of * (d + 1)]
+
+    @pl.loop(1, nh)
+    def _(d):
+        for g in range(2):
+            sum_copy(g, lax.rem(head + d, nh), head).wait_send()
 
 
 def shards(
@@ -565,11 +527,11 @@
     size = slots // CHUNKS
     duo = 2 * size
     rows_all = duo * heads
+    count = 16 * pairs
     big = 2 * pairs // 3
     small = pairs - big
     fold = max(1, 16 // small)
     fold_big = max(1, 16 // big)
-    count = 16 * pairs
     vmem = pltpu.VMEM
     dma = pltpu.SemaphoreType.DMA
     in_vmem = pl.BlockSpec(memory_space=pltpu.VMEM)
@@ -588,9 +550,9 @@
         w_uv,
         w_out,
     )
-    return pl.pallas_call(
+    result = pl.pallas_call(
         functools.partial(kernel, (nz, ny, nh)),
-        out_shape=jax.ShapeDtypeStruct((samples * ny, 2, width), BF16),
+        out_shape=jax.ShapeDtypeStruct((ny * pairs, width), BF16),
         in_specs=[in_smem] * 2 + [in_hbm] * 11,
         out_specs=in_vmem,
         scratch_shapes=[
@@ -634,18 +596,10 @@
             vmem((ny * big, heads * VDIM), F32),
             vmem((ny * small, heads * VDIM), F32),
             vmem((ny * pairs, w_out.shape[1]), F32),
-            vmem((nh, ny * big, width), F32),
-            vmem((nh, ny * small, width), F32),
             vmem((nh, ny * big, width), BF16),
             vmem((nh, ny * small, width), BF16),
-            vmem((nh // 2, ny * big, width), BF16),
-            vmem((nh // 2, ny * small, width), BF16),
-            vmem((nh // 2, ny * big, width), BF16),
-            vmem((nh // 2, ny * small, width), BF16),
-            vmem((nh // 2, ny * big, width), BF16),
-            vmem((nh // 2, ny * small, width), BF16),
-            vmem((ny * big, width), F32),
-            vmem((ny * small, width), F32),
+            vmem((nh, ny * big, width), BF16),
+            vmem((nh, ny * small, width), BF16),
             dma((len(arrays),)),
             dma((slots,)),
             dma((slots,)),
@@ -653,10 +607,8 @@
             dma((slots,)),
             dma((2, ny)),
             dma((2, ny)),
-            dma((2, nh // 2)),
-            dma((2, nh // 2)),
-            dma((2, nh // 2)),
-            dma((2, nh // 2)),
+            dma((2, nh)),
+            dma((2, nh)),
         ],
         compiler_params=pltpu.CompilerParams(
             collective_id=0, has_side_effects=True, vmem_limit_bytes=56 * 1024 * 1024
@@ -665,6 +617,7 @@
             flops=4 * 10**9, bytes_accessed=13 * 10**6, transcendentals=10**6
         ),
     )(sample_prompt, suffix_len, *arrays)
+    return result.reshape(ny * samples, 2, width)
 
 
 def solution(mesh):

time: 53.6 us -> 50.8 us (0.948)
  Pallas kernels: 51.8 us -> 49.2 us
    pallas_call x1, Pallas kernels: 51.8 us -> 49.2 us  [shards(): pl.pallas_call(functools.partial(kernel, (nz, ny, nh)), out_shape=jax.Sha...]
    unnamed x1 -> x0, local copies, waits for them, and re-layouts: 1.45 us -> none
    reshape x0 -> x1, local copies, waits for them, and re-layouts: none -> 1.45 us  [shards(): return result.reshape(ny * samples, 2, width)]
where the time goes in v6:
time: 50.8 us; the launch traced here: 50.6 us
  Pallas kernels  49.2 us (97%)
  local copies, waits for them, and re-layouts  1.45 us (3%)
    pallas_call x1, Pallas kernels, shards(): pl.pallas_call(functools.partial(kernel, (nz, ny, nh)), out_shape=jax.Sha...  49.2 us
    reshape x1, local copies, waits for them, and re-layouts, shards(): return result.reshape(ny * samples, 2, width)  1.45 us

profile of v6, /device:TPU:1, one launch (start us, length us, event | category | flops | bytes accessed | tf_op | source)
XLA Modules:
  0.0 50.6 jit_solution(2513158343374143776)
XLA Ops:
  0.0 49.2 %shard_map.127 = bf16[96,224]{1,0:T(8,128)(2,1)} custom-call(s32[12]{0:T(128)} %sp_ref.1, s32[12]{0:T(128)} %len_ref.1, bf16[12,2,1536]{2,1,0:T(2,128)(2,1)} %q_hbm.1, bf16[12,2,768]{2,1,0:T(2,128)(2,1)} %r_hbm.1, bf16[12,2,512]{2,1,0:T(2,128)(2,1)} %nl_hbm.1, bf16[12,2,64]{2,1,0:T(2,128)(2,1)} %nr_hbm.1, bf16[1,2048,512]{2,1,0:T(8,128)(2,1)} %plat_hbm.1, ...), custom_call_target="tpu_custom_call" | custom-call | flops 4000000000 | bytes 13000000 | tf_op jit(solution)/shard_map/pallas_call | solution.py:553
  49.2 1.5 %reshape.3 = bf16[48,2,224]{2,1,0:T(2,128)(2,1)} reshape(bf16[96,224]{1,0:T(8,128)(2,1)} %shard_map.127) | data formatting | bytes 86016 | tf_op jit(solution)/shard_map/reshape | solution.py:620

commit v7 on v5

--- a/solution.py
+++ b/solution.py
@@ -18,7 +18,7 @@
 FLOOR = -1e30
 SCALE = 1.0 / math.sqrt(NOPE + ROPE)
 EXP2_SCALE = SCALE * math.log2(math.e)
-CHUNKS = 2
+CHUNKS = 4
 NT = (((1,), (1,)), ((), ()))
 
 
@@ -151,11 +151,11 @@
                 (nl_hbm, nl_ref),
                 (nr_hbm, nr_ref),
                 (wuk_hbm, wuk),
-                (slat_hbm, slat),
-                (srope_hbm, srope),
                 (plat_hbm.at[0], plat),
                 (prope_hbm.at[0], prope),
                 (wuv_hbm, wuv),
+                (slat_hbm, slat),
+                (srope_hbm, srope),
                 (wout_hbm, wout),
             )
         )
@@ -197,6 +197,63 @@
     for s in range(samples):
         qb[s] = qf[2 * wide * s : 2 * wide * (s + 1), :].astype(BF16)
 
+    early = nz // 2
+
+    def local_attention():
+        for s in range(samples):
+            ntok[2 * s : 2 * s + 2, :LAT] = nl_ref[s].astype(F32)
+            ntok[2 * s : 2 * s + 2, LAT:] = jnp.zeros((2, NOPE), F32)
+            ntok[2 * s : 2 * s + 2, LAT : LAT + ROPE] = nr_ref[s].astype(F32)
+        for h in range(heads, 16):
+            lrf[pl.ds(h, pairs, stride=16), :] = jnp.zeros((pairs, NOPE), F32)
+            put(lqf, h, pairs, 16, jnp.zeros((pairs, LAT), F32))
+        for h in range(heads):
+            rows = qf[pl.ds(h, pairs, stride=wide), :].astype(BF16)
+            put(lqf, h, pairs, 16, dot(rows, wuk[h]))
+            lrf[pl.ds(h, pairs, stride=16), :] = qf[pl.ds(heads + h, pairs, stride=wide), :]
+        lane = iota((32, 128), 1)
+        for s in range(samples):
+            rows = slice(32 * s, 32 * s + 32)
+            scores = dot_nt(whole(lqf, rows).astype(BF16), slat[s]) + dot(
+                lrf[rows, :].astype(BF16)[:, :ROPE], srope[s]
+            )
+            lsc[rows, :] = jnp.where(lane < len_ref[s], scores, FLOOR)
+        new_latent = ntok[:, :LAT].astype(BF16)
+        new_rope = ntok[:, LAT:].astype(BF16)
+        count = 16 * pairs
+        new_scores = dot_nt(whole(lqf).astype(BF16), new_latent) + dot_nt(
+            lrf[...].astype(BF16), new_rope
+        )
+        row, key = iota((count, pairs), 0), iota((count, pairs), 1)
+        valid = ((key >> 1) == (row >> 5)) & ((key & 1) <= ((row >> 4) & 1))
+        new_scores = jnp.where(valid, new_scores, FLOOR)
+        old_scores = lsc[...]
+        peak = jnp.maximum(
+            jnp.max(old_scores, axis=1, keepdims=True), jnp.max(new_scores, axis=1, keepdims=True)
+        )
+        old_exp = jnp.exp2((old_scores - peak) * EXP2_SCALE)
+        new_exp = jnp.exp2((new_scores - peak) * EXP2_SCALE)
+        total = jnp.sum(old_exp, axis=1, keepdims=True) + jnp.sum(new_exp, axis=1, keepdims=True)
+        lse_col[...] = jnp.broadcast_to(peak * SCALE + jnp.log(total), lse_col.shape)
+        linv[...] = jnp.broadcast_to(1.0 / total, linv.shape)
+        lsc[...] = old_exp
+        lnew[...] = new_exp
+        new_out = dot(lnew[...].astype(BF16), ntok[:, :LAT].astype(BF16))
+        for s in range(samples):
+            rows = slice(32 * s, 32 * s + 32)
+            own_out = new_out[rows] + dot(lsc[rows, :].astype(BF16), slat[s])
+            fill(lof, own_out * linv[rows, :1], rows)
+        for h in range(heads):
+            lvf[pl.ds(h, pairs, stride=16), :] = dot(take(lof, h, pairs, 16).astype(BF16), wuv[h])
+        for h in range(heads, 16):
+            lvf[pl.ds(h, pairs, stride=16), :] = jnp.zeros((pairs, VDIM), F32)
+
+    @pl.when(z < early)
+    def _():
+        for index in (2, 3, 4, 7, 8, 9):
+            loads[index].wait()
+        local_attention()
+
     pl.semaphore_wait(barrier, slots - 1 + nh - 1)
 
     def query_copy(k):
@@ -226,52 +283,14 @@
 
     rb[0] = qb[sample_for(here)]
 
-    loads[2].wait()
-    loads[3].wait()
-    for s in range(samples):
-        ntok[2 * s : 2 * s + 2, :LAT] = nl_ref[s].astype(F32)
-        ntok[2 * s : 2 * s + 2, LAT:] = jnp.zeros((2, NOPE), F32)
-        ntok[2 * s : 2 * s + 2, LAT : LAT + ROPE] = nr_ref[s].astype(F32)
-    for h in range(heads, 16):
-        lrf[pl.ds(h, pairs, stride=16), :] = jnp.zeros((pairs, NOPE), F32)
-        put(lqf, h, pairs, 16, jnp.zeros((pairs, LAT), F32))
-    loads[4].wait()
-    for h in range(heads):
-        rows = qf[pl.ds(h, pairs, stride=wide), :].astype(BF16)
-        put(lqf, h, pairs, 16, dot(rows, wuk[h]))
-        lrf[pl.ds(h, pairs, stride=16), :] = qf[pl.ds(heads + h, pairs, stride=wide), :]
     loads[5].wait()
     loads[6].wait()
-    lane = iota((32, 128), 1)
-    for s in range(samples):
-        rows = slice(32 * s, 32 * s + 32)
-        scores = dot_nt(whole(lqf, rows).astype(BF16), slat[s]) + dot(
-            lrf[rows, :].astype(BF16)[:, :ROPE], srope[s]
-        )
-        lsc[rows, :] = jnp.where(lane < len_ref[s], scores, FLOOR)
-    new_latent = ntok[:, :LAT].astype(BF16)
-    new_rope = ntok[:, LAT:].astype(BF16)
-    count = 16 * pairs
-    new_scores = dot_nt(whole(lqf).astype(BF16), new_latent) + dot_nt(
-        lrf[...].astype(BF16), new_rope
-    )
-    row, key = iota((count, pairs), 0), iota((count, pairs), 1)
-    valid = ((key >> 1) == (row >> 5)) & ((key & 1) <= ((row >> 4) & 1))
-    new_scores = jnp.where(valid, new_scores, FLOOR)
-    old_scores = lsc[...]
-    peak = jnp.maximum(
-        jnp.max(old_scores, axis=1, keepdims=True), jnp.max(new_scores, axis=1, keepdims=True)
-    )
-    old_exp = jnp.exp2((old_scores - peak) * EXP2_SCALE)
-    new_exp = jnp.exp2((new_scores - peak) * EXP2_SCALE)
-    total = jnp.sum(old_exp, axis=1, keepdims=True) + jnp.sum(new_exp, axis=1, keepdims=True)
-    lse_col[...] = jnp.broadcast_to(peak * SCALE + jnp.log(total), lse_col.shape)
-    linv[...] = jnp.broadcast_to(1.0 / total, linv.shape)
-    lsc[...] = old_exp
-    lnew[...] = new_exp
-
-    for load in loads[7:10]:
-        load.wait()
+
+    @pl.when(z >= early)
+    def _():
+        loads[4].wait()
+        loads[7].wait()
+
     size = slots // CHUNKS
     duo = 2 * size
     rows_all = wide * size
@@ -353,15 +372,12 @@
 
     rr[here] = back[0]
 
-    new_out = dot(lnew[...].astype(BF16), ntok[:, :LAT].astype(BF16))
-    for s in range(samples):
-        rows = slice(32 * s, 32 * s + 32)
-        own_out = new_out[rows] + dot(lsc[rows, :].astype(BF16), slat[s])
-        fill(lof, own_out * linv[rows, :1], rows)
-    for h in range(heads):
-        lvf[pl.ds(h, pairs, stride=16), :] = dot(take(lof, h, pairs, 16).astype(BF16), wuv[h])
-    for h in range(heads, 16):
-        lvf[pl.ds(h, pairs, stride=16), :] = jnp.zeros((pairs, VDIM), F32)
+    @pl.when(z >= early)
+    def _():
+        for index in (2, 3, 8, 9):
+            loads[index].wait()
+        local_attention()
+
     @pl.loop(1, slots)
     def _(k):
         query_copy(k).wait_send()

time: 51.7 us -> 51.3 us (level)
  no operation moved by 1% of the time
where the time goes in v7:
time: 51.3 us; the launch traced here: 50.8 us
  Pallas kernels  49.3 us (96%)
  local copies, waits for them, and re-layouts  1.45 us (3%)
    pallas_call x1, Pallas kernels, shards(): pl.pallas_call(functools.partial(kernel, (nz, ny, nh)), out_shape=jax.Sha...  49.3 us
    reshape x1, local copies, waits for them, and re-layouts, shards(): return result.reshape(ny * samples, 2, width)  1.45 us

profile of v7, /device:TPU:1, one launch (start us, length us, event | category | flops | bytes accessed | tf_op | source)
XLA Modules:
  0.0 50.8 jit_solution(13836394491941693732)
XLA Ops:
  0.0 49.3 %shard_map.127 = bf16[96,224]{1,0:T(8,128)(2,1)} custom-call(s32[12]{0:T(128)} %sp_ref.1, s32[12]{0:T(128)} %len_ref.1, bf16[12,2,1536]{2,1,0:T(2,128)(2,1)} %q_hbm.1, bf16[12,2,768]{2,1,0:T(2,128)(2,1)} %r_hbm.1, bf16[12,2,512]{2,1,0:T(2,128)(2,1)} %nl_hbm.1, bf16[12,2,64]{2,1,0:T(2,128)(2,1)} %nr_hbm.1, bf16[1,2048,512]{2,1,0:T(8,128)(2,1)} %plat_hbm.1, ...), custom_call_target="tpu_custom_call" | custom-call | flops 4000000000 | bytes 13000000 | tf_op jit(solution)/shard_map/pallas_call | solution.py:537
  49.4 1.5 %reshape.3 = bf16[48,2,224]{2,1,0:T(2,128)(2,1)} reshape(bf16[96,224]{1,0:T(8,128)(2,1)} %shard_map.127) | data formatting | bytes 86016 | tf_op jit(solution)/shard_map/reshape | solution.py:600

commit v8 on v7

--- a/solution.py
+++ b/solution.py
@@ -445,25 +445,38 @@
             device_id_type=MESH,
         )
 
-    done = 0
+    chip, core = head // 2, lax.rem(head, 2)
+    side = chip + 1 - 2 * lax.rem(chip, 2)
+    blocks_half = nh // 2
+    columns_half = columns_all // 2
+    far = 1 - chip // 2
+    orders = (
+        (
+            2 * lax.rem(chip + 2, 4) + core,
+            2 * lax.rem(chip + 2, 4) + 1 - core,
+            2 * (3 - chip) + core,
+            2 * (3 - chip) + 1 - core,
+        ),
+        (2 * side + core, 2 * side + 1 - core, 2 * chip + 1 - core),
+    )
     tile = 256
-    for at in range(0, columns_all, tile):
-        stop = min(at + tile, columns_all)
-        part[:, at:stop] = dot(left, wout[:, at:stop])
-        while done < nh and (done + 1) * width <= stop:
-            start = done * width
+    for turn, select in enumerate((far, 1 - far)):
+        first_column = select * columns_half
+        for at in range(0, columns_half, tile):
+            stop = min(at + tile, columns_half)
+            start = pl.multiple_of(first_column + at, 128)
+            part[turn, :, at:stop] = dot(left, wout[:, pl.ds(start, stop - at)])
+        for j in range(blocks_half):
+            start = j * width
             floor = start // 128 * 128
-            ceil = min(-(-(start + width) // 128) * 128, columns_all)
-            block = part[:, floor:ceil]
+            ceil = min(-(-(start + width) // 128) * 128, columns_half)
+            block = part[turn, :, floor:ceil]
             if start > floor:
                 block = pltpu.roll(block, ceil - start, 1)
-            blocks[done] = block[:, :width].astype(BF16)
-
-            @pl.when(head != done)
-            def _(j=done):
-                sum_copy(j).start()
-
-            done += 1
+            blocks[select * blocks_half + j] = block[:, :width].astype(BF16)
+        for target in orders[turn]:
+            sum_copy(target).start()
+
     @pl.loop(1, slots)
     def _(k):
         back_copy(k).wait_send()
@@ -577,7 +590,7 @@
             vmem((count, VDIM), F32),
             vmem((ny, 2 * pairs, heads * VDIM // 2), BF16),
             vmem((ny * pairs, heads * VDIM), F32),
-            vmem((ny * pairs, w_out.shape[1]), F32),
+            vmem((2, ny * pairs, w_out.shape[1] // 2), F32),
             vmem((nh, ny * pairs, width), BF16),
             vmem((nh, ny * pairs, width), BF16),
             dma((len(arrays),)),

time: 51.3 us -> 51.4 us (level)
  no operation moved by 1% of the time
where the time goes in v8:
time: 51.4 us; the launch traced here: 51.2 us
  Pallas kernels  49.8 us (97%)
  local copies, waits for them, and re-layouts  1.45 us (3%)
    pallas_call x1, Pallas kernels, shards(): pl.pallas_call(functools.partial(kernel, (nz, ny, nh)), out_shape=jax.Sha...  49.8 us
    reshape x1, local copies, waits for them, and re-layouts, shards(): return result.reshape(ny * samples, 2, width)  1.45 us

profile of v8, /device:TPU:1, one launch (start us, length us, event | category | flops | bytes accessed | tf_op | source)
XLA Modules:
  0.0 51.2 jit_solution(12705328824753505795)
XLA Ops:
  0.0 49.8 %shard_map.127 = bf16[96,224]{1,0:T(8,128)(2,1)} custom-call(s32[12]{0:T(128)} %sp_ref.1, s32[12]{0:T(128)} %len_ref.1, bf16[12,2,1536]{2,1,0:T(2,128)(2,1)} %q_hbm.1, bf16[12,2,768]{2,1,0:T(2,128)(2,1)} %r_hbm.1, bf16[12,2,512]{2,1,0:T(2,128)(2,1)} %nl_hbm.1, bf16[12,2,64]{2,1,0:T(2,128)(2,1)} %nr_hbm.1, bf16[1,2048,512]{2,1,0:T(8,128)(2,1)} %plat_hbm.1, ...), custom_call_target="tpu_custom_call" | custom-call | flops 4000000000 | bytes 13000000 | tf_op jit(solution)/shard_map/pallas_call | solution.py:550
  49.8 1.5 %reshape.3 = bf16[48,2,224]{2,1,0:T(2,128)(2,1)} reshape(bf16[96,224]{1,0:T(8,128)(2,1)} %shard_map.127) | data formatting | bytes 86016 | tf_op jit(solution)/shard_map/reshape | solution.py:613

commit v9 on v8

--- a/solution.py
+++ b/solution.py
@@ -129,15 +129,19 @@
     y = lax.axis_index("sample")
     head = lax.axis_index("head")
     here = z * ny + y
+    own = slots - ny
+
+    def other(i):
+        return jnp.where(i <= own, i - 1, i)
 
     def ahead(k):
-        step = k // ny
+        step = nz - 1 - k // ny
         half = (step + 1) // 2
         shift = jnp.where(step % 2 == 1, half, nz - half)
         return lax.rem(z + shift, nz), lax.rem(y + k % ny, ny)
 
     def behind(k):
-        step = k // ny
+        step = nz - 1 - k // ny
         half = (step + 1) // 2
         shift = jnp.where(step % 2 == 1, nz - half, half)
         return lax.rem(z + shift, nz), lax.rem(y + ny - k % ny, ny)
@@ -165,8 +169,8 @@
     barrier = pltpu.get_barrier_semaphore()
 
     @pl.loop(1, slots)
-    def _(k):
-        to_z, to_y = ahead(k)
+    def _(i):
+        to_z, to_y = ahead(other(i))
         pl.semaphore_signal(
             barrier, inc=1, device_id={"prompt": to_z, "sample": to_y}, device_id_type=MESH
         )
@@ -276,12 +280,13 @@
         return found
 
     @pl.loop(1, slots)
-    def _(k):
+    def _(i):
+        k = other(i)
         to_z, to_y = ahead(k)
         sb[k] = qb[sample_for(to_z * ny + to_y)]
         query_copy(k).start()
 
-    rb[0] = qb[sample_for(here)]
+    rb[own] = qb[sample_for(here)]
 
     loads[5].wait()
     loads[6].wait()
@@ -314,7 +319,7 @@
 
         @pl.loop(0, size)
         def _(i):
-            @pl.when(base + i > 0)
+            @pl.when(base + i != own)
             def _():
                 query_copy(base + i).wait_recv()
 
@@ -366,11 +371,11 @@
 
         @pl.loop(0, size)
         def _(i):
-            @pl.when(base + i > 0)
+            @pl.when(base + i != own)
             def _():
                 back_copy(base + i).start()
 
-    rr[here] = back[0]
+    rr[here] = back[own]
 
     @pl.when(z >= early)
     def _():
@@ -379,14 +384,14 @@
         local_attention()
 
     @pl.loop(1, slots)
-    def _(k):
-        query_copy(k).wait_send()
+    def _(i):
+        query_copy(other(i)).wait_send()
 
     loads[10].wait()
 
     @pl.loop(1, slots)
-    def _(k):
-        back_copy(k).wait_recv()
+    def _(i):
+        back_copy(other(i)).wait_recv()
 
     for s in range(samples):
         cf[32 * s : 32 * s + 32, :] = rr[sp_ref[s]].astype(F32)
@@ -422,7 +427,7 @@
             device_id_type=MESH,
         )
 
-    for d in range(1, ny):
+    for d in sorted(range(1, ny), key=lambda d: abs(d - ny // 2)):
         value_copy(d).start()
     for d in range(1, ny):
         value_copy(d).wait_recv()
@@ -478,8 +483,8 @@
             sum_copy(target).start()
 
     @pl.loop(1, slots)
-    def _(k):
-        back_copy(k).wait_send()
+    def _(i):
+        back_copy(other(i)).wait_send()
 
     for d in range(1, ny):
         value_copy(d).wait_send()

time: 51.4 us -> 51.1 us (level)
  no operation moved by 1% of the time
where the time goes in v9:
time: 51.1 us; the launch traced here: 51 us
  Pallas kernels  49.5 us (97%)
  local copies, waits for them, and re-layouts  1.45 us (3%)
    pallas_call x1, Pallas kernels, shards(): pl.pallas_call(functools.partial(kernel, (nz, ny, nh)), out_shape=jax.Sha...  49.5 us
    reshape x1, local copies, waits for them, and re-layouts, shards(): return result.reshape(ny * samples, 2, width)  1.45 us

profile of v9, /device:TPU:1, one launch (start us, length us, event | category | flops | bytes accessed | tf_op | source)
XLA Modules:
  0.0 51.0 jit_solution(2384698847610281775)
XLA Ops:
  0.0 49.5 %shard_map.127 = bf16[96,224]{1,0:T(8,128)(2,1)} custom-call(s32[12]{0:T(128)} %sp_ref.1, s32[12]{0:T(128)} %len_ref.1, bf16[12,2,1536]{2,1,0:T(2,128)(2,1)} %q_hbm.1, bf16[12,2,768]{2,1,0:T(2,128)(2,1)} %r_hbm.1, bf16[12,2,512]{2,1,0:T(2,128)(2,1)} %nl_hbm.1, bf16[12,2,64]{2,1,0:T(2,128)(2,1)} %nr_hbm.1, bf16[1,2048,512]{2,1,0:T(8,128)(2,1)} %plat_hbm.1, ...), custom_call_target="tpu_custom_call" | custom-call | flops 4000000000 | bytes 13000000 | tf_op jit(solution)/shard_map/pallas_call | solution.py:555
  49.5 1.5 %reshape.3 = bf16[48,2,224]{2,1,0:T(2,128)(2,1)} reshape(bf16[96,224]{1,0:T(8,128)(2,1)} %shard_map.127) | data formatting | bytes 86016 | tf_op jit(solution)/shard_map/reshape | solution.py:618
